TPU v7x, 1024 devices: a whole 4x8x16 slice. The times are simulated.
1024 devices in a mesh: rep: 16 (over x, z_hi, core), fsdp: 64 (over y, z_lo).
Axes of the slice: x: 4, y: 8, z: 16 (z_hi: 2, z_lo: 8; z = z_hi * 8 + z_lo), core: 2. Of those that a mesh axis runs over, the one named last changes fastest.
Arguments:
- activations: bfloat16 [16, 16384, 4096], P('rep', 'fsdp'), may hold values from -6 to 6
- key_cotangent: bfloat16 [16, 16384, 512], P('rep', 'fsdp'), may hold values from -6 to 6
- local_params: float32 [16, 8, 131072], P('rep', None, 'fsdp'), may hold values from -6 to 6
- anchor: float32 [8, 131072], P(None, 'fsdp'), may hold values from -6 to 6
- momentum: float32 [8, 131072], P(None, 'fsdp'), may hold values from -3 to 3
- layer_fragment: int32 [8], replicated, may hold values from 0 to 3, as said below
Outputs:
- key_grad: float32 [16, 4096, 512], P('rep', 'fsdp')
- new_anchor: float32 [8, 131072], P(None, 'fsdp')
- new_momentum: float32 [8, 131072], P(None, 'fsdp')
Inputs may be any that keep to these rules, and one draw needn't show every extreme that they name: `layer_fragment`: every fragment is assigned exactly 2 layers.
All inputs are finite; a program needn't handle non-finite values.
Results may differ from a plain program's by a relative error of at most 0.0003.
Values may be sent and summed in bfloat16 or wider, within the bound.
No kernel may reach another device: no remote copies, remote signals or barrier semaphores. Data moves between devices by JAX's collectives and lax.ppermute only.
A program may use at most 64 MiB of HBM per device.

v0:
```python
import jax
import jax.numpy as jnp
from jax import lax
from jax.sharding import PartitionSpec as P

outer_rate = 0.7
momentum_keep = 0.9


def nesterov(average, anchor_rows, moment_rows):
    moved = momentum_keep * moment_rows + average
    return (anchor_rows - outer_rate * (average + momentum_keep * moved), moved)


def outer_step(delta, anchor_rows, moment_rows):
    groups = lax.axis_size("rep")
    average = lax.psum(delta, "rep") / groups
    return nesterov(average, anchor_rows, moment_rows)


def body(activations, key_cotangent, local_params, anchor, momentum, layer_fragment):
    inputs = activations[0]
    cotangent = key_cotangent[0]
    owners = lax.axis_size("fsdp")
    scale = float(inputs.shape[0] * owners) ** (-0.5)
    contract = (((0,), (0,)), ((), ()))
    grad = lax.psum_scatter(
        lax.dot_general(inputs, cotangent, contract, preferred_element_type=jnp.float32),
        "fsdp",
        scatter_dimension=0,
        tiled=True,
    )
    key_grad = (grad * scale)[None]
    chosen = layer_fragment == 0
    delta = anchor - local_params[0]
    spread_anchor, spread_moment = outer_step(delta, anchor, momentum)
    mask = chosen[:, None]
    new_anchor = jnp.where(mask, spread_anchor, anchor)
    new_momentum = jnp.where(mask, spread_moment, momentum)
    return (key_grad, new_anchor, new_momentum)


def solution(mesh):
    placed = (
        P("rep", "fsdp", None),
        P("rep", "fsdp", None),
        P("rep", None, "fsdp"),
        P(None, "fsdp"),
        P(None, "fsdp"),
        P(),
    )
    return jax.shard_map(
        body,
        mesh=mesh,
        in_specs=placed,
        out_specs=(P("rep", "fsdp", None), P(None, "fsdp"), P(None, "fsdp")),
        check_vma=False,
    )
```

profile of v0, /device:TPU:6, one launch (start us, length us, event | category | flops | bytes accessed | tf_op | source)
XLA Modules:
  0.0 530.4 jit_solution(14016057489729471935)
XLA Ops:
  8.0 0.0 copy-start
  8.0 0.0 all-reduce.2.cloned.1.call-start
  8.1 1.6 bitcast_subtract_fusion
  9.7 0.0 all-reduce.2.cloned.1.call-update
  9.7 0.0 reduce-scatter.2.cloned.1.call-start
  9.8 0.0 copy-done
  9.8 5.5 %fusion = f32[4096,512]{1,0:T(8,128)} fusion(bf16[1,256,4096]{2,1,0:T(8,128)(2,1)S(1)} %copy-done, bf16[1,256,512]{2,1,0:T(8,128)(2,1)} %param.7), kind=kOutput, calls=%fused_computation | convolution fusion | flops 1073741824 | bytes 10747904 | tf_op jit(solution)/shard_map/dot_general | solution.py:28
  15.3 0.0 copy-start.3
  15.3 0.0 copy-start.1
  15.3 0.0 copy-start.2
  15.3 0.0 reduce-scatter.2.cloned.1.call-update
  15.3 0.6 copy-done.3
  15.9 248.6 %all-reduce.2.cloned.1.call-done = f32[8,2048]{1,0:T(8,128)} async-done(((f32[8,2048]{1,0:T(8,128)}), f32[8,2048]{1,0:T(8,128)}) %all-reduce.2.cloned.1.call-update) | async-done | bytes 65552 | tf_op jit(solution)/shard_map/psum | solution.py:17
  264.5 0.0 copy-done.1
  264.5 0.0 copy-done.2
  264.5 1.6 fusion.3
  266.1 255.3 %reduce-scatter.2.cloned.1.call-done = f32[64,512]{1,0:T(8,128)} async-done(((f32[4096,512]{1,0:T(8,128)}), f32[64,512]{1,0:T(8,128)}) %reduce-scatter.2.cloned.1.call-update) | async-done | bytes 131088 | tf_op jit(solution)/shard_map/reduce_scatter | solution.py:27
  521.4 1.6 multiply_bitcast_fusion
  (1 shorter events, 0.0 us)
Async XLA Ops:
  8.0 1.8 copy-start
  8.0 256.5 %all-reduce.2.cloned.1.call-start = ((), (), s32[]{:S(2)}) async-start(), calls=%async_computation.2 | async-start | bytes 131072 | tf_op jit(solution)/shard_map/psum | solution.py:17
  9.7 511.6 %reduce-scatter.2.cloned.1.call-start = ((), (), s32[]{:S(2)}) async-start(), calls=%async_computation.1 | async-start | bytes 8519680 | tf_op jit(solution)/shard_map/reduce_scatter | solution.py:27
  15.3 0.7 copy-start.3
  15.3 249.2 %copy-start.1 = (f32[8,2048]{1,0:T(8,128)S(1)}, f32[8,2048]{1,0:T(8,128)}, u32[]{:S(2)}) copy-start(f32[8,2048]{1,0:T(8,128)} %param.9) | copy-start | bytes 196612
  15.3 249.2 %copy-start.2 = (f32[8,2048]{1,0:T(8,128)S(1)}, f32[8,2048]{1,0:T(8,128)}, u32[]{:S(2)}) copy-start(f32[8,2048]{1,0:T(8,128)} %param.10) | copy-start | bytes 196612
Sparse Core Ops, SparseCore 0:
  12.9 251.5 all-reduce.1
Sparse Core Ops, SparseCore 1:
  15.4 505.9 reduce-scatter.1
where the time goes:
time: 531 us; the launch traced here: 530 us
  waiting for transfers between devices  504 us (95%)
  between operations  15.5 us (3%)
  matrix products  5.47 us (1%)
    reduce_scatter x1, waiting for transfers between devices, body(): lax.psum_scatter(lax.dot_general(inputs, cotangent, contract, preferred_e...  255 us
    psum x1, waiting for transfers between devices, outer_step(): average = lax.psum(delta, 'rep') / groups  249 us
  transfers between devices with their start and end apart: 2, of which 2 were waited for; matrix products, arithmetic and copies ran while one was open for 1% of the time, Pallas kernels for 0%

commit v1 on v0

v1 whole, which is shorter than its diff:
```python
import functools
import math

import jax
import jax.numpy as jnp
from jax import lax
from jax.experimental import pallas as pl
from jax.experimental.pallas import tpu as pltpu
from jax.sharding import PartitionSpec as P

outer_rate = 0.7
momentum_keep = 0.9
ring, line = 8, 8
group = 64
tail = 16
steps_per_octave = 8.0
top = 32760.0
whole = pl.BlockSpec(memory_space=pltpu.VMEM)
limit = pltpu.CompilerParams(vmem_limit_bytes=40 * 1024 * 1024)


def code(values, out, at=None):
    count = values.shape[0] // group
    exponents = []
    for g in range(count):
        part = values[g * group:(g + 1) * group]
        most = jnp.max(jnp.abs(part), axis=0, keepdims=True)
        exponent = jnp.ceil(jnp.log(jnp.maximum(most, 1e-30)) * (steps_per_octave / math.log(2.0))) + 1.0
        inverse = jnp.exp(exponent * (-math.log(2.0) / steps_per_octave)) * top
        magic = 12582912.0
        coded = (part * inverse + magic) - magic
        out[g * group:(g + 1) * group, :] = coded.astype(jnp.int32).astype(jnp.int16)
        exponents.append(exponent)
    exponents.append(jnp.zeros((tail - count, values.shape[1]), jnp.float32))
    out[count * group:count * group + tail, :] = jnp.concatenate(exponents, axis=0).astype(jnp.int32).astype(jnp.int16)


def scales(message):
    rows = message.shape[0] - tail
    exponents = message[rows:rows + tail, :].astype(jnp.int32).astype(jnp.float32)
    return jnp.exp(exponents * (math.log(2.0) / steps_per_octave)) * (1.0 / top)


def decoded(message, scale, g):
    return message[g * group:(g + 1) * group, :].astype(jnp.int32).astype(jnp.float32) * scale[g:g + 1]


def product(left, right):
    return lax.dot_general(left, right, (((0,), (0,)), ((), ())), preferred_element_type=jnp.float32)


def sums_kernel(place, own_here, own_up, own_down, cotangent, from_below, from_above, up, down, here):
    width = own_here.shape[1]
    half = width // 2
    mine = cotangent[...]
    keys = from_below.shape[1] - mine.shape[1]
    below = from_below[:, keys:]
    above = from_above[:, keys:]
    here[...] = (
        product(own_here[...], mine)
        + product(from_below[:, :width], below)
        + product(from_above[:, :width], above)
    )
    rest = product(own_up[...], mine) + product(from_above[:, width:2 * width], above)
    first = product(from_below[:, 2 * width:keys], below)
    code(jnp.concatenate([rest[:half] + first, rest[half:]], axis=0), up)
    rest = product(own_down[...], mine) + product(from_below[:, width:2 * width], below)
    last = product(from_above[:, 2 * width:keys], above)
    code(jnp.concatenate([rest[:half], rest[half:] + last], axis=0), down)


def sums(place, activations, cotangent, from_below, from_above):
    tokens, width = cotangent.shape[0], activations.shape[1] // ring
    columns = cotangent.shape[1]

    def block(shift):
        return pl.BlockSpec((tokens, width), lambda i, place: (0, lax.rem(place[0] + shift + ring, ring)))

    full = lambda a: pl.BlockSpec(a.shape, lambda i, place: (0, 0))
    outs = [
        jax.ShapeDtypeStruct((width + tail, columns), jnp.int16),
        jax.ShapeDtypeStruct((width + tail, columns), jnp.int16),
        jax.ShapeDtypeStruct((width, columns), jnp.float32),
    ]
    return pl.pallas_call(
        sums_kernel,
        out_shape=outs,
        grid_spec=pltpu.PrefetchScalarGridSpec(
            num_scalar_prefetch=1,
            grid=(1,),
            in_specs=[block(0), block(3), block(-3), full(cotangent), full(from_below), full(from_above)],
            out_specs=[full(o) for o in outs],
        ),
        compiler_params=limit,
    )(place, activations, activations, activations, cotangent, from_below, from_above)


def fold_kernel(arrived, bit, *refs):
    place, kept = refs[0], refs[1]
    messages = refs[2:2 + arrived]
    sent, out, total = refs[2 + arrived:]
    factors = [scales(m) for m in messages]
    count = kept.shape[0] // group
    side = place[0]
    for g in range(count):
        value = kept[g * group:(g + 1) * group, :]
        for m, f in zip(messages, factors):
            value = value + decoded(m, f, g)
        total[g % 2, (g // 2) * group:(g // 2 + 1) * group, :] = value
    out[...] = total[side]
    code(total[1 - side], sent)


def fold(side, kept, messages):
    rows, columns = kept.shape
    outs = [
        jax.ShapeDtypeStruct((rows // 2 + tail, columns), jnp.int16),
        jax.ShapeDtypeStruct((rows // 2, columns), jnp.float32),
    ]
    return pl.pallas_call(
        functools.partial(fold_kernel, len(messages), None),
        out_shape=outs,
        in_specs=[pl.BlockSpec(memory_space=pltpu.SMEM)] + [whole] * (1 + len(messages)),
        out_specs=[whole, whole],
        scratch_shapes=[pltpu.VMEM((2, rows // 2, columns), jnp.float32)],
        compiler_params=limit,
    )(side, kept, *messages)


def last_kernel(scale, kept, message, out):
    out[...] = (kept[...] + decoded(message, scales(message), 0)) * scale


def last(scale, kept, message):
    return pl.pallas_call(
        functools.partial(last_kernel, scale),
        out_shape=jax.ShapeDtypeStruct(kept.shape, jnp.float32),
        in_specs=[whole, whole],
        out_specs=whole,
        compiler_params=limit,
    )(kept, message)


def along_ring(shift):
    return [(y * line + z, ((y + shift) % ring) * line + z) for y in range(ring) for z in range(line)]


def along_line(bit):
    return [(y * line + z, y * line + (z ^ bit)) for y in range(ring) for z in range(line)]


def gradient(inputs, cotangent):
    tokens, features = inputs.shape
    width = features // ring
    at = lax.axis_index("fsdp")
    y, z = at // line, at % line

    def chunk(shift, start=0, size=width):
        return lax.dynamic_slice_in_dim(inputs, lax.rem(y + shift + ring, ring) * width + start, size, 1)

    half = width // 2
    with jax.named_scope("inputs_to_neighbours"):
        above = jnp.concatenate([chunk(1), chunk(-2), chunk(4, 0, half), cotangent], axis=1)
        below = jnp.concatenate([chunk(-1), chunk(2), chunk(4, half, half), cotangent], axis=1)
        from_below = lax.ppermute(above, "fsdp", along_ring(1))
        from_above = lax.ppermute(below, "fsdp", along_ring(-1))
    place = jnp.full((1,), y, jnp.int32)
    up, down, here = sums(place, inputs, cotangent, from_below, from_above)
    with jax.named_scope("sums_along_ring"):
        messages = [lax.ppermute(up, "fsdp", along_ring(3)), lax.ppermute(down, "fsdp", along_ring(-3))]
    kept = here
    bit = 1
    while bit < line:
        side = jnp.full((1,), (z // bit) % 2, jnp.int32)
        sent, kept = fold(side, kept, messages)
        with jax.named_scope("sums_along_line"):
            messages = [lax.ppermute(sent, "fsdp", along_line(bit))]
        bit *= 2
    return last(float(tokens * ring * line) ** (-0.5), kept, messages[0])


def outer_step(local, anchor, momentum, layer_fragment):
    groups = lax.axis_size("rep")
    chosen = layer_fragment == 0
    order = jnp.cumsum(chosen.astype(jnp.int32))
    picks = [(chosen & (order == i + 1))[:, None] for i in range(2)]
    delta = anchor - local
    total = jnp.stack([jnp.sum(jnp.where(p, delta, 0.0), axis=0) for p in picks])
    with jax.named_scope("differences_over_replicas"):
        bit = 1
        while bit < groups:
            total = total + lax.ppermute(total, "rep", [(r, r ^ bit) for r in range(groups)])
            bit *= 2
    average = total / groups
    average = jnp.where(picks[0], average[0:1], average[1:2])
    moved = momentum_keep * momentum + average
    mask = chosen[:, None]
    new_anchor = jnp.where(mask, anchor - outer_rate * (average + momentum_keep * moved), anchor)
    return new_anchor, jnp.where(mask, moved, momentum)


def body(activations, key_cotangent, local_params, anchor, momentum, layer_fragment):
    key_grad = gradient(activations[0], key_cotangent[0])[None]
    new_anchor, new_momentum = outer_step(local_params[0], anchor, momentum, layer_fragment)
    return (key_grad, new_anchor, new_momentum)


def solution(mesh):
    placed = (
        P("rep", "fsdp", None),
        P("rep", "fsdp", None),
        P("rep", None, "fsdp"),
        P(None, "fsdp"),
        P(None, "fsdp"),
        P(),
    )
    return jax.shard_map(
        body,
        mesh=mesh,
        in_specs=placed,
        out_specs=(P("rep", "fsdp", None), P(None, "fsdp"), P(None, "fsdp")),
        check_vma=False,
    )
```

time: 531 us -> 125 us (0.24)
  the two profiles are of different devices: /device:TPU:6 before, /device:TPU:16 now
where the time goes in v1:
time: 125 us
  starting transfers between devices  66.7 us (53%)
  waiting for transfers between devices  44.7 us (36%)
  Pallas kernels  5.29 us (4%)
  local copies, waits for them, and re-layouts  4.45 us (4%)
  other arithmetic  2.52 us (2%)
    ppermute x4, starting transfers between devices, outer_step(): lax.ppermute(total, 'rep', [(r, r ^ bit) for r in range(groups)])  28.9 us
    ppermute x3, starting transfers between devices, gradient(): messages = [lax.ppermute(sent, 'fsdp', along_line(bit))]  22.3 us
    ppermute x3, waiting for transfers between devices, gradient(): messages = [lax.ppermute(sent, 'fsdp', along_line(bit))]  17.8 us
    ppermute x1, waiting for transfers between devices, gradient(): from_below = lax.ppermute(above, 'fsdp', along_ring(1))  16 us
    ppermute x1, starting transfers between devices, gradient(): lax.ppermute(down, 'fsdp', along_ring(-3))  5.78 us
    ppermute x4, waiting for transfers between devices, outer_step(): lax.ppermute(total, 'rep', [(r, r ^ bit) for r in range(groups)])  3.94 us
    ppermute x1, starting transfers between devices, gradient(): lax.ppermute(up, 'fsdp', along_ring(3))  3.86 us
    pallas_call x1, Pallas kernels, sums(): pl.pallas_call(sums_kernel, out_shape=outs, grid_spec=pltpu.PrefetchScala...  3.81 us
  transfers between devices with their start and end apart: 11, of which 8 were waited for; matrix products, arithmetic and copies ran while one was open for 1% of the time, Pallas kernels for 3%

profile of v1, /device:TPU:16, one launch (start us, length us, event | category | flops | bytes accessed | tf_op | source)
XLA Modules:
  0.0 124.6 jit_solution(7099649083169390973)
XLA Ops:
  0.6 0.0 copy-start.1
  0.7 1.0 dynamic-slice_bitcast_fusion.4
  1.7 1.3 %dynamic-slice_bitcast_fusion.1 = (bf16[256,512]{1,0:T(8,128)(2,1)S(1)}, bf16[256,512]{1,0:T(8,128)(2,1)S(1)}, bf16[256,512]{1,0:T(8,128)(2,1)S(1)}, bf16[256,512]{1,0:T(8,128)(2,1)S(1)}) fusion(bf16[1,256,4096]{2,1,0:T(8,128)(2,1)} %param.6, s32[]{:T(128)S(6)} %select_n.76, s32[]{:T(128)S(6)} %select_n.74, s32[]{:T(128)S(6)} %select_n.73, s32[]{:T(128)S(6)} %select_n.77), kind=kLoop, calls=%fused_computation.3 | loop fusion | bytes 2097168 | tf_op jit(solution)/shard_map/inputs_to_neighbours/dynamic_slice | solution.py:159
  3.0 0.0 copy-start.7
  3.0 0.0 copy-start.4
  3.0 0.0 copy-start.6
  3.0 0.0 copy-start
  3.0 0.0 copy-done.1
  3.1 1.4 %pad_maximum_fusion = (bf16[256,1792]{1,0:T(8,128)(2,1)}, bf16[256,1792]{1,0:T(8,128)(2,1)}) fusion(bf16[256,512]{1,0:T(8,128)(2,1)S(1)} %bitcast.38, bf16[256,256]{1,0:T(8,128)(2,1)S(1)} %get-tuple-element.27, bf16[256,512]{1,0:T(8,128)(2,1)S(1)} %get-tuple-element.26, bf16[256,512]{1,0:T(8,128)(2,1)S(1)} %get-tuple-element.23, ...), kind=kLoop, calls=%fused_computation | loop fusion | flops 6881280 | bytes 3407872 | tf_op jit(solution)/shard_map/inputs_to_neighbours/concatenate | solution.py:164
  4.4 3.5 %collective-permute-start = (bf16[256,1792]{1,0:T(8,128)(2,1)}, bf16[256,1792]{1,0:T(8,128)(2,1)S(1)}, u32[]{:S(2)}, u32[]{:S(2)}) collective-permute-start(bf16[256,1792]{1,0:T(8,128)(2,1)} %get-tuple-element.30), channel_id=1, source_target_pairs={{0,8},{1,9},{2,10},{3,11},{4,12},{5,13},{6,14},{7,15},{8,16},{9,17... | collective-permute-start | bytes 2752520 | tf_op jit(solution)/shard_map/inputs_to_neighbours/ppermute | solution.py:165
  7.9 2.4 %collective-permute-start.1 = (bf16[256,1792]{1,0:T(8,128)(2,1)}, bf16[256,1792]{1,0:T(8,128)(2,1)}, u32[]{:S(2)}, u32[]{:S(2)}) collective-permute-start(bf16[256,1792]{1,0:T(8,128)(2,1)} %get-tuple-element.29), channel_id=1, source_target_pairs={{0,56},{1,57},{2,58},{3,59},{4,60},{5,61},{6,62},{7,63},{8,0},{9,1... | collective-permute-start | bytes 2752520 | tf_op jit(solution)/shard_map/inputs_to_neighbours/ppermute | solution.py:166
  10.3 0.0 copy-done.7
  10.3 0.2 reduce-window.9
  10.5 0.0 copy-done.4
  10.5 0.0 copy-done.6
  10.5 0.1 select_reduce_fusion.1
  10.6 1.9 %collective-permute-start.7 = (f32[2,2048]{1,0:T(2,128)S(1)}, f32[2,2048]{1,0:T(2,128)S(1)}, u32[]{:S(2)}, u32[]{:S(2)}) collective-permute-start(f32[2,2048]{1,0:T(2,128)S(1)} %pad_maximum_fusion.2), channel_id=1, source_target_pairs={{0,64},{64,0},{128,192},{192,128},{256,320},{320,256},{384,448},{4... | collective-permute-start | bytes 49160 | tf_op jit(solution)/shard_map/differences_over_replicas/ppermute | solution.py:192
  12.6 16.0 %collective-permute-done.from_below = bf16[256,1792]{1,0:T(8,128)(2,1)S(1)} collective-permute-done((bf16[256,1792]{1,0:T(8,128)(2,1)}, bf16[256,1792]{1,0:T(8,128)(2,1)S(1)}, u32[]{:S(2)}, u32[]{:S(2)}) %collective-permute-start) | collective-permute-done | bytes 917536 | tf_op jit(solution)/shard_map/inputs_to_neighbours/ppermute | solution.py:165
  28.6 0.0 copy-start.2
  28.6 0.9 copy-done.2
  29.6 3.4 %collective-permute-done.1.from_above = bf16[256,1792]{1,0:T(8,128)(2,1)} collective-permute-done((bf16[256,1792]{1,0:T(8,128)(2,1)}, bf16[256,1792]{1,0:T(8,128)(2,1)}, u32[]{:S(2)}, u32[]{:S(2)}) %collective-permute-start.1) | collective-permute-done | bytes 917536 | tf_op jit(solution)/shard_map/inputs_to_neighbours/ppermute | solution.py:166
  33.0 0.0 copy-done
  33.0 0.0 copy-start.3
  33.0 1.2 copy-done.3
  34.2 3.8 %shard_map.85 = (s16[528,512]{1,0:T(8,128)(2,1)}, s16[528,512]{1,0:T(8,128)(2,1)}, f32[512,512]{1,0:T(8,128)S(1)}) custom-call(s32[1]{0:T(128)} %bitcast.3.place, bf16[256,4096]{1,0:T(8,128)(2,1)S(1)} %bitcast.35, bf16[256,4096]{1,0:T(8,128)(2,1)S(1)} %bitcast.36, bf16[256,4096]{1,0:T(8,128)(2,1)S(1)} %bitcast.37, bf16[256,512]{1,0:T(8,128)(2,1)S(1)} %bitcast.39, ...), custom_call_target="tpu_custom_call" | custom-call | tf_op jit(solution)/shard_map/pallas_call | solution.py:85
  38.0 3.9 %collective-permute-start.2 = (s16[528,512]{1,0:T(8,128)(2,1)}, s16[528,512]{1,0:T(8,128)(2,1)S(1)}, u32[]{:S(2)}, u32[]{:S(2)}) collective-permute-start(s16[528,512]{1,0:T(8,128)(2,1)} %get-tuple-element.13), channel_id=1, source_target_pairs={{0,24},{1,25},{2,26},{3,27},{4,28},{5,29},{6,30},{7,31},{8,32},{9,... | collective-permute-start | bytes 1622024 | tf_op jit(solution)/shard_map/sums_along_ring/ppermute | solution.py:170
  41.8 5.8 %collective-permute-start.3 = (s16[528,512]{1,0:T(8,128)(2,1)}, s16[528,512]{1,0:T(8,128)(2,1)S(1)}, u32[]{:S(2)}, u32[]{:S(2)}) collective-permute-start(s16[528,512]{1,0:T(8,128)(2,1)} %get-tuple-element.14), channel_id=1, source_target_pairs={{0,40},{1,41},{2,42},{3,43},{4,44},{5,45},{6,46},{7,47},{8,48},{9,... | collective-permute-start | bytes 1622024 | tf_op jit(solution)/shard_map/sums_along_ring/ppermute | solution.py:170
  47.6 0.0 collective-permute-done.7
  47.7 0.0 copy-start.5
  47.7 18.7 %collective-permute-start.8 = (f32[2,2048]{1,0:T(2,128)S(1)}, f32[2,2048]{1,0:T(2,128)S(1)}, u32[]{:S(2)}, u32[]{:S(2)}) collective-permute-start(f32[2,2048]{1,0:T(2,128)S(1)} %fusion.2), channel_id=1, source_target_pairs={{0,128},{64,192},{128,0},{192,64},{256,384},{320,448},{384,256},{4... | collective-permute-start | bytes 49160 | tf_op jit(solution)/shard_map/differences_over_replicas/ppermute | solution.py:192
  66.4 1.7 %collective-permute-done.8 = f32[2,2048]{1,0:T(2,128)S(1)} collective-permute-done((f32[2,2048]{1,0:T(2,128)S(1)}, f32[2,2048]{1,0:T(2,128)S(1)}, u32[]{:S(2)}, u32[]{:S(2)}) %collective-permute-start.8) | collective-permute-done | bytes 16416 | tf_op jit(solution)/shard_map/differences_over_replicas/ppermute | solution.py:192
  68.1 3.4 %collective-permute-start.9 = (f32[2,2048]{1,0:T(2,128)S(1)}, f32[2,2048]{1,0:T(2,128)S(1)}, u32[]{:S(2)}, u32[]{:S(2)}) collective-permute-start(f32[2,2048]{1,0:T(2,128)S(1)} %fusion.4), channel_id=1, source_target_pairs={{0,256},{64,320},{128,384},{192,448},{256,0},{320,64},{384,128},{4... | collective-permute-start | bytes 49160 | tf_op jit(solution)/shard_map/differences_over_replicas/ppermute | solution.py:192
  71.5 2.2 %collective-permute-done.9 = f32[2,2048]{1,0:T(2,128)S(1)} collective-permute-done((f32[2,2048]{1,0:T(2,128)S(1)}, f32[2,2048]{1,0:T(2,128)S(1)}, u32[]{:S(2)}, u32[]{:S(2)}) %collective-permute-start.9) | collective-permute-done | bytes 16416 | tf_op jit(solution)/shard_map/differences_over_replicas/ppermute | solution.py:192
  73.8 4.9 %collective-permute-start.10 = (f32[2,2048]{1,0:T(2,128)S(1)}, f32[2,2048]{1,0:T(2,128)S(1)}, u32[]{:S(2)}, u32[]{:S(2)}) collective-permute-start(f32[2,2048]{1,0:T(2,128)S(1)} %add.108), channel_id=1, source_target_pairs={{0,512},{64,576},{128,640},{192,704},{256,768},{320,832},{384,896}... | collective-permute-start | bytes 49160 | tf_op jit(solution)/shard_map/differences_over_replicas/ppermute | solution.py:192
  78.8 0.0 collective-permute-done.2.refs_2_
  78.8 3.4 %collective-permute-done.3.refs_3_ = s16[528,512]{1,0:T(8,128)(2,1)S(1)} collective-permute-done((s16[528,512]{1,0:T(8,128)(2,1)}, s16[528,512]{1,0:T(8,128)(2,1)S(1)}, u32[]{:S(2)}, u32[]{:S(2)}) %collective-permute-start.3) | collective-permute-done | bytes 540704 | tf_op jit(solution)/shard_map/sums_along_ring/ppermute | solution.py:170
  82.2 0.5 shard_map.86
  82.7 4.7 %collective-permute-start.4 = (s16[272,512]{1,0:T(8,128)(2,1)S(1)}, s16[272,512]{1,0:T(8,128)(2,1)S(1)}, u32[]{:S(2)}, u32[]{:S(2)}) collective-permute-start(s16[272,512]{1,0:T(8,128)(2,1)S(1)} %get-tuple-element.16), channel_id=1, source_target_pairs={{0,1},{1,0},{2,3},{3,2},{4,5},{5,4},{6,7},{7,6},{8,9},{9,8},{10,11... | collective-permute-start | bytes 835592 | tf_op jit(solution)/shard_map/sums_along_line/ppermute | solution.py:177
  87.5 0.0 collective-permute-done.10
  87.5 6.1 %collective-permute-done.4.refs_2_ = s16[272,512]{1,0:T(8,128)(2,1)S(1)} collective-permute-done((s16[272,512]{1,0:T(8,128)(2,1)S(1)}, s16[272,512]{1,0:T(8,128)(2,1)S(1)}, u32[]{:S(2)}, u32[]{:S(2)}) %collective-permute-start.4) | collective-permute-done | bytes 278560 | tf_op jit(solution)/shard_map/sums_along_line/ppermute | solution.py:177
  93.6 0.2 shard_map.87
  93.8 6.6 %collective-permute-start.5 = (s16[144,512]{1,0:T(8,128)(2,1)S(1)}, s16[144,512]{1,0:T(8,128)(2,1)S(1)}, u32[]{:S(2)}, u32[]{:S(2)}) collective-permute-start(s16[144,512]{1,0:T(8,128)(2,1)S(1)} %get-tuple-element.18), channel_id=1, source_target_pairs={{0,2},{1,3},{2,0},{3,1},{4,6},{5,7},{6,4},{7,5},{8,10},{9,11},{10,... | collective-permute-start | bytes 442376 | tf_op jit(solution)/shard_map/sums_along_line/ppermute | solution.py:177
  100.4 6.4 %collective-permute-done.5.refs_2_ = s16[144,512]{1,0:T(8,128)(2,1)S(1)} collective-permute-done((s16[144,512]{1,0:T(8,128)(2,1)S(1)}, s16[144,512]{1,0:T(8,128)(2,1)S(1)}, u32[]{:S(2)}, u32[]{:S(2)}) %collective-permute-start.5) | collective-permute-done | bytes 147488 | tf_op jit(solution)/shard_map/sums_along_line/ppermute | solution.py:177
  106.8 0.1 shard_map.88
  106.9 10.9 %collective-permute-start.6 = (s16[80,512]{1,0:T(8,128)(2,1)S(1)}, s16[80,512]{1,0:T(8,128)(2,1)S(1)}, u32[]{:S(2)}, u32[]{:S(2)}) collective-permute-start(s16[80,512]{1,0:T(8,128)(2,1)S(1)} %get-tuple-element.20), channel_id=1, source_target_pairs={{0,4},{1,5},{2,6},{3,7},{4,0},{5,1},{6,2},{7,3},{8,12},{9,13},{10,... | collective-permute-start | bytes 245768 | tf_op jit(solution)/shard_map/sums_along_line/ppermute | solution.py:177
  117.9 0.0 copy-done.5
  117.9 0.7 fusion.1
  118.6 5.3 %collective-permute-done.6.message = s16[80,512]{1,0:T(8,128)(2,1)S(1)} collective-permute-done((s16[80,512]{1,0:T(8,128)(2,1)S(1)}, s16[80,512]{1,0:T(8,128)(2,1)S(1)}, u32[]{:S(2)}, u32[]{:S(2)}) %collective-permute-start.6) | collective-permute-done | bytes 81952 | tf_op jit(solution)/shard_map/sums_along_line/ppermute | solution.py:177
  124.0 0.7 shard_map.89
  (8 shorter events, 0.1 us)
Async XLA Ops:
  0.6 2.4 %copy-start.1 = (bf16[1,256,512]{2,1,0:T(8,128)(2,1)S(1)}, bf16[1,256,512]{2,1,0:T(8,128)(2,1)}, u32[]{:S(2)}) copy-start(bf16[1,256,512]{2,1,0:T(8,128)(2,1)} %param.7) | copy-start | bytes 786436
  3.0 7.3 %copy-start.7 = (s32[8]{0:T(128)S(1)}, s32[8]{0:T(128)}, u32[]{:S(2)}) copy-start(s32[8]{0:T(128)} %param.11) | copy-start | bytes 100
  3.0 7.5 %copy-start.4 = (f32[8,2048]{1,0:T(8,128)S(1)}, f32[8,2048]{1,0:T(8,128)}, u32[]{:S(2)}) copy-start(f32[8,2048]{1,0:T(8,128)} %param.9) | copy-start | bytes 196612
  3.0 7.5 %copy-start.6 = (f32[1,8,2048]{2,1,0:T(8,128)S(1)}, f32[1,8,2048]{2,1,0:T(8,128)}, u32[]{:S(2)}) copy-start(f32[1,8,2048]{2,1,0:T(8,128)} %param.8) | copy-start | bytes 196612
  3.0 30.0 %copy-start = (bf16[1,256,4096]{2,1,0:T(8,128)(2,1)S(1)}, bf16[1,256,4096]{2,1,0:T(8,128)(2,1)}, u32[]{:S(2)}) copy-start(bf16[1,256,4096]{2,1,0:T(8,128)(2,1)} %param.6) | copy-start | bytes 6291460
  4.4 24.2 %collective-permute-start = (bf16[256,1792]{1,0:T(8,128)(2,1)}, bf16[256,1792]{1,0:T(8,128)(2,1)S(1)}, u32[]{:S(2)}, u32[]{:S(2)}) collective-permute-start(bf16[256,1792]{1,0:T(8,128)(2,1)} %get-tuple-element.30), channel_id=1, source_target_pairs={{0,8},{1,9},{2,10},{3,11},{4,12},{5,13},{6,14},{7,15},{8,16},{9,17... | collective-permute-start | bytes 2752520 | tf_op jit(solution)/shard_map/inputs_to_neighbours/ppermute | solution.py:165
  7.9 25.1 %collective-permute-start.1 = (bf16[256,1792]{1,0:T(8,128)(2,1)}, bf16[256,1792]{1,0:T(8,128)(2,1)}, u32[]{:S(2)}, u32[]{:S(2)}) collective-permute-start(bf16[256,1792]{1,0:T(8,128)(2,1)} %get-tuple-element.29), channel_id=1, source_target_pairs={{0,56},{1,57},{2,58},{3,59},{4,60},{5,61},{6,62},{7,63},{8,0},{9,1... | collective-permute-start | bytes 2752520 | tf_op jit(solution)/shard_map/inputs_to_neighbours/ppermute | solution.py:166
  10.6 37.0 %collective-permute-start.7 = (f32[2,2048]{1,0:T(2,128)S(1)}, f32[2,2048]{1,0:T(2,128)S(1)}, u32[]{:S(2)}, u32[]{:S(2)}) collective-permute-start(f32[2,2048]{1,0:T(2,128)S(1)} %pad_maximum_fusion.2), channel_id=1, source_target_pairs={{0,64},{64,0},{128,192},{192,128},{256,320},{320,256},{384,448},{4... | collective-permute-start | bytes 49160 | tf_op jit(solution)/shard_map/differences_over_replicas/ppermute | solution.py:192
  28.6 0.9 copy-start.2
  33.0 1.2 copy-start.3
  38.0 40.8 %collective-permute-start.2 = (s16[528,512]{1,0:T(8,128)(2,1)}, s16[528,512]{1,0:T(8,128)(2,1)S(1)}, u32[]{:S(2)}, u32[]{:S(2)}) collective-permute-start(s16[528,512]{1,0:T(8,128)(2,1)} %get-tuple-element.13), channel_id=1, source_target_pairs={{0,24},{1,25},{2,26},{3,27},{4,28},{5,29},{6,30},{7,31},{8,32},{9,... | collective-permute-start | bytes 1622024 | tf_op jit(solution)/shard_map/sums_along_ring/ppermute | solution.py:170
  41.8 40.4 %collective-permute-start.3 = (s16[528,512]{1,0:T(8,128)(2,1)}, s16[528,512]{1,0:T(8,128)(2,1)S(1)}, u32[]{:S(2)}, u32[]{:S(2)}) collective-permute-start(s16[528,512]{1,0:T(8,128)(2,1)} %get-tuple-element.14), channel_id=1, source_target_pairs={{0,40},{1,41},{2,42},{3,43},{4,44},{5,45},{6,46},{7,47},{8,48},{9,... | collective-permute-start | bytes 1622024 | tf_op jit(solution)/shard_map/sums_along_ring/ppermute | solution.py:170
  47.7 70.2 %copy-start.5 = (f32[8,2048]{1,0:T(8,128)S(1)}, f32[8,2048]{1,0:T(8,128)}, u32[]{:S(2)}) copy-start(f32[8,2048]{1,0:T(8,128)} %param.10) | copy-start | bytes 196612
  47.7 20.4 %collective-permute-start.8 = (f32[2,2048]{1,0:T(2,128)S(1)}, f32[2,2048]{1,0:T(2,128)S(1)}, u32[]{:S(2)}, u32[]{:S(2)}) collective-permute-start(f32[2,2048]{1,0:T(2,128)S(1)} %fusion.2), channel_id=1, source_target_pairs={{0,128},{64,192},{128,0},{192,64},{256,384},{320,448},{384,256},{4... | collective-permute-start | bytes 49160 | tf_op jit(solution)/shard_map/differences_over_replicas/ppermute | solution.py:192
  68.1 5.6 %collective-permute-start.9 = (f32[2,2048]{1,0:T(2,128)S(1)}, f32[2,2048]{1,0:T(2,128)S(1)}, u32[]{:S(2)}, u32[]{:S(2)}) collective-permute-start(f32[2,2048]{1,0:T(2,128)S(1)} %fusion.4), channel_id=1, source_target_pairs={{0,256},{64,320},{128,384},{192,448},{256,0},{320,64},{384,128},{4... | collective-permute-start | bytes 49160 | tf_op jit(solution)/shard_map/differences_over_replicas/ppermute | solution.py:192
  73.8 13.7 %collective-permute-start.10 = (f32[2,2048]{1,0:T(2,128)S(1)}, f32[2,2048]{1,0:T(2,128)S(1)}, u32[]{:S(2)}, u32[]{:S(2)}) collective-permute-start(f32[2,2048]{1,0:T(2,128)S(1)} %add.108), channel_id=1, source_target_pairs={{0,512},{64,576},{128,640},{192,704},{256,768},{320,832},{384,896}... | collective-permute-start | bytes 49160 | tf_op jit(solution)/shard_map/differences_over_replicas/ppermute | solution.py:192
  82.7 10.9 %collective-permute-start.4 = (s16[272,512]{1,0:T(8,128)(2,1)S(1)}, s16[272,512]{1,0:T(8,128)(2,1)S(1)}, u32[]{:S(2)}, u32[]{:S(2)}) collective-permute-start(s16[272,512]{1,0:T(8,128)(2,1)S(1)} %get-tuple-element.16), channel_id=1, source_target_pairs={{0,1},{1,0},{2,3},{3,2},{4,5},{5,4},{6,7},{7,6},{8,9},{9,8},{10,11... | collective-permute-start | bytes 835592 | tf_op jit(solution)/shard_map/sums_along_line/ppermute | solution.py:177
  93.8 13.0 %collective-permute-start.5 = (s16[144,512]{1,0:T(8,128)(2,1)S(1)}, s16[144,512]{1,0:T(8,128)(2,1)S(1)}, u32[]{:S(2)}, u32[]{:S(2)}) collective-permute-start(s16[144,512]{1,0:T(8,128)(2,1)S(1)} %get-tuple-element.18), channel_id=1, source_target_pairs={{0,2},{1,3},{2,0},{3,1},{4,6},{5,7},{6,4},{7,5},{8,10},{9,11},{10,... | collective-permute-start | bytes 442376 | tf_op jit(solution)/shard_map/sums_along_line/ppermute | solution.py:177
  106.9 17.0 %collective-permute-start.6 = (s16[80,512]{1,0:T(8,128)(2,1)S(1)}, s16[80,512]{1,0:T(8,128)(2,1)S(1)}, u32[]{:S(2)}, u32[]{:S(2)}) collective-permute-start(s16[80,512]{1,0:T(8,128)(2,1)S(1)} %get-tuple-element.20), channel_id=1, source_target_pairs={{0,4},{1,5},{2,6},{3,7},{4,0},{5,1},{6,2},{7,3},{8,12},{9,13},{10,... | collective-permute-start | bytes 245768 | tf_op jit(solution)/shard_map/sums_along_line/ppermute | solution.py:177

commit v2 on v0

v2 whole, which is shorter than its diff:
```python
import functools
import math

import jax
import jax.numpy as jnp
from jax import lax
from jax.experimental import pallas as pl
from jax.experimental.pallas import tpu as pltpu
from jax.sharding import PartitionSpec as P

outer_rate = 0.7
momentum_keep = 0.9
ring, line = 8, 8
group = 64
tail = 16
steps_per_octave = 8.0
top = 32760.0
whole = pl.BlockSpec(memory_space=pltpu.VMEM)
anywhere = pl.BlockSpec(memory_space=pl.ANY)
limit = pltpu.CompilerParams(vmem_limit_bytes=40 * 1024 * 1024)


def work(micros):
    return pl.CostEstimate(flops=0, bytes_accessed=micros * 3000000, transcendentals=0)


def code(values, out):
    count = values.shape[0] // group
    exponents = []
    for g in range(count):
        part = values[g * group:(g + 1) * group, :]
        most = jnp.max(jnp.abs(part), axis=0, keepdims=True)
        exponent = jnp.ceil(jnp.log(jnp.maximum(most, 1e-30)) * (steps_per_octave / math.log(2.0))) + 1.0
        inverse = jnp.exp(exponent * (-math.log(2.0) / steps_per_octave)) * top
        magic = 12582912.0
        coded = (part * inverse + magic) - magic
        out[g * group:(g + 1) * group, :] = coded.astype(jnp.int32).astype(jnp.int16)
        exponents.append(exponent)
    exponents.append(jnp.zeros((tail - count, values.shape[1]), jnp.float32))
    out[count * group:count * group + tail, :] = jnp.concatenate(exponents, axis=0).astype(jnp.int32).astype(jnp.int16)


def scales(message):
    rows = message.shape[0] - tail
    exponents = message[rows:rows + tail, :].astype(jnp.int32).astype(jnp.float32)
    return jnp.exp(exponents * (math.log(2.0) / steps_per_octave)) * (1.0 / top)


def decoded(message, scale, g):
    return message[g * group:(g + 1) * group, :].astype(jnp.int32).astype(jnp.float32) * scale[g:g + 1]


def product(left, right):
    return lax.dot_general(left, right, (((0,), (0,)), ((), ())), preferred_element_type=jnp.float32)


def chunk_of(activations, shift):
    width = activations.shape[1] // ring
    return pl.BlockSpec((activations.shape[0], width), lambda i, place: (0, lax.rem(place[0] + shift + ring, ring)))


def on_chunks(kernel, place, inputs, outs, scratch=(), mebibytes=40):
    full = lambda a: pl.BlockSpec(a.shape, lambda i, place: (0, 0))
    specs = [chunk_of(*a) if isinstance(a, tuple) else full(a) for a in inputs]
    return pl.pallas_call(
        kernel,
        out_shape=outs,
        grid_spec=pltpu.PrefetchScalarGridSpec(
            num_scalar_prefetch=1,
            grid=(1,),
            in_specs=specs,
            out_specs=[full(o) for o in outs],
            scratch_shapes=[pltpu.VMEM(shape, jnp.float32) for shape in scratch],
        ),
        compiler_params=pltpu.CompilerParams(vmem_limit_bytes=mebibytes * 1024 * 1024),
        cost_estimate=work(1),
    )(place, *[a[0] if isinstance(a, tuple) else a for a in inputs])


def pack_kernel(place, next_up, next_down, up, down, across, cotangent, above, below):
    width = up.shape[1]
    half = width // 2
    above[:, :width] = next_up[...]
    below[:, :width] = next_down[...]
    above[:, width:2 * width] = down[...]
    below[:, width:2 * width] = up[...]
    above[:, 2 * width:2 * width + half] = across[:, :half]
    below[:, 2 * width:2 * width + half] = across[:, half:]
    above[:, 2 * width + half:] = cotangent[...]
    below[:, 2 * width + half:] = cotangent[...]


def pack(place, activations, cotangent):
    columns = activations.shape[1] // ring * 5 // 2 + cotangent.shape[1]
    out = jax.ShapeDtypeStruct((activations.shape[0], columns), activations.dtype)
    inputs = [(activations, shift) for shift in (1, -1, 2, -2, 4)] + [cotangent]
    return on_chunks(pack_kernel, place, inputs, [out, out], mebibytes=60)


def part(source, total, side, kept, sent):
    for g in range(source.shape[0] // group):
        total[g % 2, g // 2 * group:(g // 2 + 1) * group, :] = source[g * group:(g + 1) * group, :]
    kept[...] = total[side]
    code(total.at[1 - side], sent)


def sums_kernel(place, own, own_up, own_down, cotangent, below, above, far_sent, far_kept, near_sent, near_kept,
                far, near, far_parted, near_parted):
    width = own.shape[1]
    half = width // 2
    keys = 2 * width + half
    mine, under, over = cotangent[...], below[:, keys:], above[:, keys:]
    far[:width] = product(own_up[...], mine) + product(above[:, width:2 * width], over)
    far[:half] += product(below[:, 2 * width:keys], under)
    far[width:] = product(own_down[...], mine) + product(below[:, width:2 * width], under)
    far[width + half:] += product(above[:, 2 * width:keys], over)
    part(far, far_parted, place[1], far_kept, far_sent)
    near[...] = product(own[...], mine) + product(below[:, :width], under) + product(above[:, :width], over)
    part(near, near_parted, place[1], near_kept, near_sent)


def sums(place, activations, cotangent, from_below, from_above):
    width = activations.shape[1] // ring
    half = width // 2
    columns = cotangent.shape[1]
    outs = [
        jax.ShapeDtypeStruct((width + tail, columns), jnp.int16),
        jax.ShapeDtypeStruct((width, columns), jnp.float32),
        jax.ShapeDtypeStruct((half + tail, columns), jnp.int16),
        jax.ShapeDtypeStruct((half, columns), jnp.float32),
    ]
    inputs = [(activations, 0), (activations, 3), (activations, -3), cotangent, from_below, from_above]
    scratch = [(2 * width, columns), (width, columns), (2, width, columns), (2, half, columns)]
    return on_chunks(sums_kernel, place, inputs, outs, scratch)


def call(kernel, outs, place, *args, scratch=(), micros=1):
    return pl.pallas_call(
        kernel,
        out_shape=[jax.ShapeDtypeStruct(s, d) for s, d in outs],
        in_specs=[pl.BlockSpec(memory_space=pltpu.SMEM)] + [whole] * len(args),
        out_specs=[whole] * len(outs),
        scratch_shapes=[pltpu.VMEM(s, jnp.float32) for s in scratch],
        compiler_params=limit,
        cost_estimate=work(micros),
    )(place, *args)


def rest_kernel(place, kept, message, up, down, sums):
    scale = scales(message)
    for g in range(kept.shape[0] // group):
        sums[g * group:(g + 1) * group, :] = kept[g * group:(g + 1) * group, :] + decoded(message, scale, g)
    rows = kept.shape[0] // 2
    code(sums.at[:rows], up)
    code(sums.at[rows:], down)


def rest(place, kept, message):
    rows, columns = kept.shape
    coded = ((rows // 2 + tail, columns), jnp.int16)
    return call(rest_kernel, [coded, coded], place, kept, message, scratch=[(rows, columns)], micros=5)


def fold_kernel(bit, place, kept, *refs):
    messages, (sent, out, total) = refs[:-3], refs[-3:]
    factors = [scales(m) for m in messages]
    for g in range(kept.shape[0] // group):
        value = kept[g * group:(g + 1) * group, :]
        for m, factor in zip(messages, factors):
            value = value + decoded(m, factor, g)
        total[g % 2, g // 2 * group:(g // 2 + 1) * group, :] = value
    side = place[bit]
    out[...] = total[side]
    code(total.at[1 - side], sent)


def fold(place, bit, kept, messages, micros=1):
    half, columns = kept.shape[0] // 2, kept.shape[1]
    outs = [((half + tail, columns), jnp.int16), ((half, columns), jnp.float32)]
    return call(functools.partial(fold_kernel, bit), outs, place, kept, *messages, scratch=[(2, half, columns)], micros=micros)


def last_kernel(scale, place, kept, message, out):
    out[...] = (kept[...] + decoded(message, scales(message), 0)) * scale


def last(scale, place, kept, message):
    return call(functools.partial(last_kernel, scale), [(kept.shape, jnp.float32)], place, kept, message)[0]


def along_ring(shift):
    return [(y * line + z, ((y + shift) % ring) * line + z) for y in range(ring) for z in range(line)]


def along_line(bit):
    return [(y * line + z, y * line + (z ^ bit)) for y in range(ring) for z in range(line)]


def after(value, *others):
    return lax.optimization_barrier((value, *others))[0]


def outer_sums(local, anchor, layer_fragment):
    chosen = layer_fragment == 0
    order = jnp.cumsum(chosen.astype(jnp.int32))
    picks = [(chosen & (order == i + 1))[:, None] for i in range(2)]
    delta = anchor - local
    total = jnp.stack([jnp.sum(jnp.where(p, delta, 0.0), axis=0) for p in picks])
    groups = lax.axis_size("rep")

    def add_over(total, bit):
        with jax.named_scope("differences_over_replicas"):
            return total + lax.ppermute(total, "rep", [(r, r ^ bit) for r in range(groups)])

    return picks, total, add_over


def outer_step(picks, total, anchor, momentum):
    average = total / lax.axis_size("rep")
    average = jnp.where(picks[0], average[0:1], average[1:2])
    moved = momentum_keep * momentum + average
    mask = picks[0] | picks[1]
    new_anchor = jnp.where(mask, anchor - outer_rate * (average + momentum_keep * moved), anchor)
    return new_anchor, jnp.where(mask, moved, momentum)


def step(inputs, cotangent, local, anchor, momentum, layer_fragment):
    tokens, features = inputs.shape
    at = lax.axis_index("fsdp")
    y, z = lax.div(at, line), lax.rem(at, line)
    place = jnp.stack([y, lax.rem(z, 2), lax.rem(lax.div(z, 2), 2), lax.div(z, 4)]).astype(jnp.int32)

    def ring_move(a, shift):
        return lax.ppermute(a, "fsdp", along_ring(shift))

    def line_move(a, bit):
        return lax.ppermute(a, "fsdp", along_line(bit))

    with jax.named_scope("inputs_to_neighbours"):
        above, below = pack(place, inputs, cotangent)
        received = [ring_move(above, 1), ring_move(below, -1)]
    picks, total, add_over = outer_sums(local, anchor, layer_fragment)
    total = add_over(add_over(after(total, above), 2), 4)
    sent, kept, near, here = sums(after(place, total), inputs, cotangent, *received)
    with jax.named_scope("along_line_first"):
        arrived = line_move(sent, 1)
        messages = [line_move(near, 1)]
    total = add_over(add_over(after(total, sent), 1), 8)
    up, down = rest(after(place, total), kept, arrived)
    with jax.named_scope("far_along_ring"):
        messages += [ring_move(up, 3), ring_move(down, -3)]
    with jax.named_scope("along_line"):
        sent, here = fold(place, 2, here, messages)
        sent = line_move(sent, 2)
        sent, here = fold(place, 3, here, [sent])
        sent = line_move(sent, 4)
    grad = last(float(tokens * ring * line) ** (-0.5), place, here, sent)
    return (grad, *outer_step(picks, total, anchor, momentum))


def body(activations, key_cotangent, local_params, anchor, momentum, layer_fragment):
    grad, new_anchor, new_momentum = step(
        activations[0], key_cotangent[0], local_params[0], anchor, momentum, layer_fragment
    )
    return (grad[None], new_anchor, new_momentum)


def solution(mesh):
    placed = (
        P("rep", "fsdp", None),
        P("rep", "fsdp", None),
        P("rep", None, "fsdp"),
        P(None, "fsdp"),
        P(None, "fsdp"),
        P(),
    )
    return jax.shard_map(
        body,
        mesh=mesh,
        in_specs=placed,
        out_specs=(P("rep", "fsdp", None), P(None, "fsdp"), P(None, "fsdp")),
        check_vma=False,
    )
```

time: 531 us -> 116 us (0.22)
  the two profiles are of different devices: /device:TPU:6 before, /device:TPU:16 now
where the time goes in v2:
time: 116 us; the launch traced here: 115 us
  starting transfers between devices  61.6 us (53%)
  waiting for transfers between devices  40 us (34%)
  Pallas kernels  10.8 us (9%)
  other arithmetic  1.71 us (1%)
    ppermute x4, starting transfers between devices, add_over(): lax.ppermute(total, 'rep', [(r, r ^ bit) for r in range(groups)])  29.6 us
    ppermute x4, waiting for transfers between devices, ring_move(): return lax.ppermute(a, 'fsdp', along_ring(shift))  21.6 us
    ppermute x4, starting transfers between devices, line_move(): return lax.ppermute(a, 'fsdp', along_line(bit))  17.1 us
    ppermute x4, starting transfers between devices, ring_move(): return lax.ppermute(a, 'fsdp', along_ring(shift))  14.8 us
    ppermute x4, waiting for transfers between devices, line_move(): return lax.ppermute(a, 'fsdp', along_line(bit))  13.3 us
    pallas_call x2, Pallas kernels, on_chunks(): pl.pallas_call(kernel, out_shape=outs, grid_spec=pltpu.PrefetchScalarGrid...  7.06 us
    ppermute x4, waiting for transfers between devices, add_over(): lax.ppermute(total, 'rep', [(r, r ^ bit) for r in range(groups)])  5.09 us
    pallas_call x4, Pallas kernels, call(): pl.pallas_call(kernel, out_shape=[jax.ShapeDtypeStruct(s, d) for s, d in...  3.77 us
  transfers between devices with their start and end apart: 12, of which 7 were waited for; matrix products, arithmetic and copies ran while one was open for 1% of the time, Pallas kernels for 1%

profile of v2, /device:TPU:16, one launch (start us, length us, event | category | flops | bytes accessed | tf_op | source)
XLA Modules:
  0.0 115.1 jit_solution(2578377435954738966)
XLA Ops:
  0.7 0.6 pad_add_fusion.place
  1.3 0.0 copy-start.6
  1.3 0.0 copy-start.3
  1.3 0.0 copy-start.5
  1.3 0.0 copy-start
  1.3 0.0 copy-start.1
  1.3 0.0 copy-start.2
  1.3 3.5 %inputs_to_neighbours.1 = (bf16[256,1792]{1,0:T(8,128)(2,1)}, bf16[256,1792]{1,0:T(8,128)(2,1)}) custom-call(s32[4]{0:T(128)} %pad_add_fusion.place, bf16[256,4096]{1,0:T(8,128)(2,1)} %bitcast.25, bf16[256,4096]{1,0:T(8,128)(2,1)} %bitcast.26, bf16[256,4096]{1,0:T(8,128)(2,1)} %bitcast.27, bf16[256,4096]{1,0:T(8,128)(2,1)} %bitcast.28, ...), custom_call_target="tpu_custom_call" | custom-call | bytes 3000000 | tf_op jit(solution)/shard_map/inputs_to_neighbours/pallas_call | solution.py:65
  4.8 2.3 %collective-permute-start.3 = (bf16[256,1792]{1,0:T(8,128)(2,1)}, bf16[256,1792]{1,0:T(8,128)(2,1)S(1)}, u32[]{:S(2)}, u32[]{:S(2)}) collective-permute-start(bf16[256,1792]{1,0:T(8,128)(2,1)} %get-tuple-element.22), channel_id=1, source_target_pairs={{0,56},{1,57},{2,58},{3,59},{4,60},{5,61},{6,62},{7,63},{8,0},{9,1... | collective-permute-start | bytes 2752520 | tf_op jit(solution)/shard_map/inputs_to_neighbours/ppermute | solution.py:234
  7.2 3.5 %collective-permute-start.2 = (bf16[256,1792]{1,0:T(8,128)(2,1)}, bf16[256,1792]{1,0:T(8,128)(2,1)}, u32[]{:S(2)}, u32[]{:S(2)}) collective-permute-start(bf16[256,1792]{1,0:T(8,128)(2,1)} %get-tuple-element.19), channel_id=1, source_target_pairs={{0,8},{1,9},{2,10},{3,11},{4,12},{5,13},{6,14},{7,15},{8,16},{9,17... | collective-permute-start | bytes 2752520 | tf_op jit(solution)/shard_map/inputs_to_neighbours/ppermute | solution.py:234
  10.7 0.0 copy-done.6
  10.7 0.2 reduce-window.9
  10.9 0.0 copy-done.3
  10.9 0.0 copy-done.5
  10.9 0.1 select_reduce_fusion.1
  11.0 19.4 %collective-permute-start = (f32[2,2048]{1,0:T(2,128)S(1)}, f32[2,2048]{1,0:T(2,128)S(1)}, u32[]{:S(2)}, u32[]{:S(2)}) collective-permute-start(f32[2,2048]{1,0:T(2,128)S(1)} %pad_maximum_fusion), channel_id=1, source_target_pairs={{0,128},{64,192},{128,0},{192,64},{256,384},{320,448},{384,256},{4... | collective-permute-start | bytes 49160 | tf_op jit(solution)/shard_map/differences_over_replicas/ppermute | solution.py:213
  30.4 1.7 %collective-permute-done = f32[2,2048]{1,0:T(2,128)S(1)} collective-permute-done((f32[2,2048]{1,0:T(2,128)S(1)}, f32[2,2048]{1,0:T(2,128)S(1)}, u32[]{:S(2)}, u32[]{:S(2)}) %collective-permute-start) | collective-permute-done | bytes 16416 | tf_op jit(solution)/shard_map/differences_over_replicas/ppermute | solution.py:213
  32.1 3.4 %collective-permute-start.1 = (f32[2,2048]{1,0:T(2,128)S(1)}, f32[2,2048]{1,0:T(2,128)S(1)}, u32[]{:S(2)}, u32[]{:S(2)}) collective-permute-start(f32[2,2048]{1,0:T(2,128)S(1)} %add.18), channel_id=1, source_target_pairs={{0,256},{64,320},{128,384},{192,448},{256,0},{320,64},{384,128},{4... | collective-permute-start | bytes 49160 | tf_op jit(solution)/shard_map/differences_over_replicas/ppermute | solution.py:213
  35.5 2.2 %collective-permute-done.1 = f32[2,2048]{1,0:T(2,128)S(1)} collective-permute-done((f32[2,2048]{1,0:T(2,128)S(1)}, f32[2,2048]{1,0:T(2,128)S(1)}, u32[]{:S(2)}, u32[]{:S(2)}) %collective-permute-start.1) | collective-permute-done | bytes 16416 | tf_op jit(solution)/shard_map/differences_over_replicas/ppermute | solution.py:213
  37.8 0.0 collective-permute-done.3.above
  37.8 0.0 collective-permute-done.2.below
  37.8 0.0 copy-done
  37.8 0.0 copy-done.1
  37.8 0.0 copy-done.2
  37.8 3.5 %shard_map.85 = (s16[528,512]{1,0:T(8,128)(2,1)S(1)}, f32[512,512]{1,0:T(8,128)S(1)}, s16[272,512]{1,0:T(8,128)(2,1)S(1)}, f32[256,512]{1,0:T(8,128)S(1)}) custom-call(s32[4]{0:T(128)S(1)} %copy-done.2, bf16[256,4096]{1,0:T(8,128)(2,1)S(1)} %bitcast.30, bf16[256,4096]{1,0:T(8,128)(2,1)S(1)} %bitcast.31, bf16[256,4096]{1,0:T(8,128)(2,1)S(1)} %bitcast.32, ...), custom_call_target="tpu_custom_call" | custom-call | bytes 3000000 | tf_op jit(solution)/shard_map/pallas_call | solution.py:65
  41.4 0.0 copy-start.4
  41.4 3.5 %collective-permute-start.7 = (s16[528,512]{1,0:T(8,128)(2,1)S(1)}, s16[528,512]{1,0:T(8,128)(2,1)S(1)}, u32[]{:S(2)}, u32[]{:S(2)}) collective-permute-start(s16[528,512]{1,0:T(8,128)(2,1)S(1)} %get-tuple-element.25), channel_id=1, source_target_pairs={{0,1},{1,0},{2,3},{3,2},{4,5},{5,4},{6,7},{7,6},{8,9},{9,8},{10,11... | collective-permute-start | bytes 1622024 | tf_op jit(solution)/shard_map/along_line_first/ppermute | solution.py:237
  44.9 1.9 %collective-permute-start.5 = (f32[2,2048]{1,0:T(2,128)S(1)}, f32[2,2048]{1,0:T(2,128)S(1)}, u32[]{:S(2)}, u32[]{:S(2)}) collective-permute-start(f32[2,2048]{1,0:T(2,128)S(1)} %add.19), channel_id=1, source_target_pairs={{0,64},{64,0},{128,192},{192,128},{256,320},{320,256},{384,448},{4... | collective-permute-start | bytes 49160 | tf_op jit(solution)/shard_map/differences_over_replicas/ppermute | solution.py:213
  46.8 1.1 collective-permute-done.5
  48.0 4.9 %collective-permute-start.6 = (f32[2,2048]{1,0:T(2,128)S(1)}, f32[2,2048]{1,0:T(2,128)S(1)}, u32[]{:S(2)}, u32[]{:S(2)}) collective-permute-start(f32[2,2048]{1,0:T(2,128)S(1)} %add.20), channel_id=1, source_target_pairs={{0,512},{64,576},{128,640},{192,704},{256,768},{320,832},{384,896}... | collective-permute-start | bytes 49160 | tf_op jit(solution)/shard_map/differences_over_replicas/ppermute | solution.py:213
  52.9 2.5 %collective-permute-start.4 = (s16[272,512]{1,0:T(8,128)(2,1)S(1)}, s16[272,512]{1,0:T(8,128)(2,1)S(1)}, u32[]{:S(2)}, u32[]{:S(2)}) collective-permute-start(s16[272,512]{1,0:T(8,128)(2,1)S(1)} %get-tuple-element.24), channel_id=1, source_target_pairs={{0,1},{1,0},{2,3},{3,2},{4,5},{5,4},{6,7},{7,6},{8,9},{9,8},{10,11... | collective-permute-start | bytes 835592 | tf_op jit(solution)/shard_map/along_line_first/ppermute | solution.py:237
  55.4 0.0 collective-permute-done.6
  55.4 0.0 collective-permute-done.7.message
  55.4 1.0 shard_map.86
  56.5 5.8 %collective-permute-start.8 = (s16[272,512]{1,0:T(8,128)(2,1)S(1)}, s16[272,512]{1,0:T(8,128)(2,1)S(1)}, u32[]{:S(2)}, u32[]{:S(2)}) collective-permute-start(s16[272,512]{1,0:T(8,128)(2,1)S(1)} %get-tuple-element.29), channel_id=1, source_target_pairs={{0,24},{1,25},{2,26},{3,27},{4,28},{5,29},{6,30},{7,31},{8,32},{9,... | collective-permute-start | bytes 835592 | tf_op jit(solution)/shard_map/far_along_ring/ppermute | solution.py:234
  62.3 3.2 %collective-permute-start.9 = (s16[272,512]{1,0:T(8,128)(2,1)S(1)}, s16[272,512]{1,0:T(8,128)(2,1)S(1)}, u32[]{:S(2)}, u32[]{:S(2)}) collective-permute-start(s16[272,512]{1,0:T(8,128)(2,1)S(1)} %get-tuple-element.30), channel_id=1, source_target_pairs={{0,40},{1,41},{2,42},{3,43},{4,44},{5,45},{6,46},{7,47},{8,48},{9,... | collective-permute-start | bytes 835592 | tf_op jit(solution)/shard_map/far_along_ring/ppermute | solution.py:234
  65.5 0.0 collective-permute-done.4.refs_0_
  65.5 14.5 %collective-permute-done.8.refs_1_ = s16[272,512]{1,0:T(8,128)(2,1)S(1)} collective-permute-done((s16[272,512]{1,0:T(8,128)(2,1)S(1)}, s16[272,512]{1,0:T(8,128)(2,1)S(1)}, u32[]{:S(2)}, u32[]{:S(2)}) %collective-permute-start.8) | collective-permute-done | bytes 278560 | tf_op jit(solution)/shard_map/far_along_ring/ppermute | solution.py:234
  80.0 7.1 %collective-permute-done.9.refs_2_ = s16[272,512]{1,0:T(8,128)(2,1)S(1)} collective-permute-done((s16[272,512]{1,0:T(8,128)(2,1)S(1)}, s16[272,512]{1,0:T(8,128)(2,1)S(1)}, u32[]{:S(2)}, u32[]{:S(2)}) %collective-permute-start.9) | collective-permute-done | bytes 278560 | tf_op jit(solution)/shard_map/far_along_ring/ppermute | solution.py:234
  87.0 0.9 along_line.2
  87.9 4.4 %collective-permute-start.10 = (s16[144,512]{1,0:T(8,128)(2,1)S(1)}, s16[144,512]{1,0:T(8,128)(2,1)S(1)}, u32[]{:S(2)}, u32[]{:S(2)}) collective-permute-start(s16[144,512]{1,0:T(8,128)(2,1)S(1)} %get-tuple-element.32), channel_id=1, source_target_pairs={{0,2},{1,3},{2,0},{3,1},{4,6},{5,7},{6,4},{7,5},{8,10},{9,11},{10,... | collective-permute-start | bytes 442376 | tf_op jit(solution)/shard_map/along_line/ppermute | solution.py:237
  92.4 7.2 %collective-permute-done.10.refs_0_ = s16[144,512]{1,0:T(8,128)(2,1)S(1)} collective-permute-done((s16[144,512]{1,0:T(8,128)(2,1)S(1)}, s16[144,512]{1,0:T(8,128)(2,1)S(1)}, u32[]{:S(2)}, u32[]{:S(2)}) %collective-permute-start.10) | collective-permute-done | bytes 147488 | tf_op jit(solution)/shard_map/along_line/ppermute | solution.py:237
  99.5 0.6 along_line.3
  100.2 6.8 %collective-permute-start.11 = (s16[80,512]{1,0:T(8,128)(2,1)S(1)}, s16[80,512]{1,0:T(8,128)(2,1)S(1)}, u32[]{:S(2)}, u32[]{:S(2)}) collective-permute-start(s16[80,512]{1,0:T(8,128)(2,1)S(1)} %get-tuple-element.34), channel_id=1, source_target_pairs={{0,4},{1,5},{2,6},{3,7},{4,0},{5,1},{6,2},{7,3},{8,12},{9,13},{10,... | collective-permute-start | bytes 245768 | tf_op jit(solution)/shard_map/along_line/ppermute | solution.py:237
  107.0 0.0 copy-done.4
  107.0 0.7 fusion.1
  107.7 6.1 %collective-permute-done.11.message = s16[80,512]{1,0:T(8,128)(2,1)S(1)} collective-permute-done((s16[80,512]{1,0:T(8,128)(2,1)S(1)}, s16[80,512]{1,0:T(8,128)(2,1)S(1)}, u32[]{:S(2)}, u32[]{:S(2)}) %collective-permute-start.11) | collective-permute-done | bytes 81952 | tf_op jit(solution)/shard_map/along_line/ppermute | solution.py:237
  113.9 1.2 %shard_map.87 = f32[64,512]{1,0:T(8,128)} custom-call(s32[4]{0:T(128)S(1)} %copy-done.2, f32[64,512]{1,0:T(8,128)S(1)} %get-tuple-element.33.kept, s16[80,512]{1,0:T(8,128)(2,1)S(1)} %collective-permute-done.11.message), custom_call_target="tpu_custom_call" | custom-call | bytes 3000000 | tf_op jit(solution)/shard_map/pallas_call | solution.py:138
  (8 shorter events, 0.1 us)
Async XLA Ops:
  1.3 9.4 %copy-start.6 = (s32[8]{0:T(128)S(1)}, s32[8]{0:T(128)}, u32[]{:S(2)}) copy-start(s32[8]{0:T(128)} %param.11) | copy-start | bytes 100
  1.3 9.6 %copy-start.3 = (f32[8,2048]{1,0:T(8,128)S(1)}, f32[8,2048]{1,0:T(8,128)}, u32[]{:S(2)}) copy-start(f32[8,2048]{1,0:T(8,128)} %param.9) | copy-start | bytes 196612
  1.3 9.6 %copy-start.5 = (f32[1,8,2048]{2,1,0:T(8,128)S(1)}, f32[1,8,2048]{2,1,0:T(8,128)}, u32[]{:S(2)}) copy-start(f32[1,8,2048]{2,1,0:T(8,128)} %param.8) | copy-start | bytes 196612
  1.3 36.5 %copy-start = (bf16[1,256,4096]{2,1,0:T(8,128)(2,1)S(1)}, bf16[1,256,4096]{2,1,0:T(8,128)(2,1)}, u32[]{:S(2)}) copy-start(bf16[1,256,4096]{2,1,0:T(8,128)(2,1)} %param.6) | copy-start | bytes 6291460
  1.3 36.6 %copy-start.1 = (bf16[1,256,512]{2,1,0:T(8,128)(2,1)S(1)}, bf16[1,256,512]{2,1,0:T(8,128)(2,1)}, u32[]{:S(2)}) copy-start(bf16[1,256,512]{2,1,0:T(8,128)(2,1)} %param.7) | copy-start | bytes 786436
  1.3 36.6 %copy-start.2 = (s32[4]{0:T(128)S(1)}, s32[4]{0:T(128)}, u32[]{:S(2)}) copy-start(s32[4]{0:T(128)} %pad_add_fusion.place) | copy-start | bytes 52
  4.8 33.0 %collective-permute-start.3 = (bf16[256,1792]{1,0:T(8,128)(2,1)}, bf16[256,1792]{1,0:T(8,128)(2,1)S(1)}, u32[]{:S(2)}, u32[]{:S(2)}) collective-permute-start(bf16[256,1792]{1,0:T(8,128)(2,1)} %get-tuple-element.22), channel_id=1, source_target_pairs={{0,56},{1,57},{2,58},{3,59},{4,60},{5,61},{6,62},{7,63},{8,0},{9,1... | collective-permute-start | bytes 2752520 | tf_op jit(solution)/shard_map/inputs_to_neighbours/ppermute | solution.py:234
  7.2 30.6 %collective-permute-start.2 = (bf16[256,1792]{1,0:T(8,128)(2,1)}, bf16[256,1792]{1,0:T(8,128)(2,1)}, u32[]{:S(2)}, u32[]{:S(2)}) collective-permute-start(bf16[256,1792]{1,0:T(8,128)(2,1)} %get-tuple-element.19), channel_id=1, source_target_pairs={{0,8},{1,9},{2,10},{3,11},{4,12},{5,13},{6,14},{7,15},{8,16},{9,17... | collective-permute-start | bytes 2752520 | tf_op jit(solution)/shard_map/inputs_to_neighbours/ppermute | solution.py:234
  11.0 21.1 %collective-permute-start = (f32[2,2048]{1,0:T(2,128)S(1)}, f32[2,2048]{1,0:T(2,128)S(1)}, u32[]{:S(2)}, u32[]{:S(2)}) collective-permute-start(f32[2,2048]{1,0:T(2,128)S(1)} %pad_maximum_fusion), channel_id=1, source_target_pairs={{0,128},{64,192},{128,0},{192,64},{256,384},{320,448},{384,256},{4... | collective-permute-start | bytes 49160 | tf_op jit(solution)/shard_map/differences_over_replicas/ppermute | solution.py:213
  32.1 5.6 %collective-permute-start.1 = (f32[2,2048]{1,0:T(2,128)S(1)}, f32[2,2048]{1,0:T(2,128)S(1)}, u32[]{:S(2)}, u32[]{:S(2)}) collective-permute-start(f32[2,2048]{1,0:T(2,128)S(1)} %add.18), channel_id=1, source_target_pairs={{0,256},{64,320},{128,384},{192,448},{256,0},{320,64},{384,128},{4... | collective-permute-start | bytes 49160 | tf_op jit(solution)/shard_map/differences_over_replicas/ppermute | solution.py:213
  41.4 65.6 %copy-start.4 = (f32[8,2048]{1,0:T(8,128)S(1)}, f32[8,2048]{1,0:T(8,128)}, u32[]{:S(2)}) copy-start(f32[8,2048]{1,0:T(8,128)} %param.10) | copy-start | bytes 196612
  41.4 14.1 %collective-permute-start.7 = (s16[528,512]{1,0:T(8,128)(2,1)S(1)}, s16[528,512]{1,0:T(8,128)(2,1)S(1)}, u32[]{:S(2)}, u32[]{:S(2)}) collective-permute-start(s16[528,512]{1,0:T(8,128)(2,1)S(1)} %get-tuple-element.25), channel_id=1, source_target_pairs={{0,1},{1,0},{2,3},{3,2},{4,5},{5,4},{6,7},{7,6},{8,9},{9,8},{10,11... | collective-permute-start | bytes 1622024 | tf_op jit(solution)/shard_map/along_line_first/ppermute | solution.py:237
  44.9 3.1 %collective-permute-start.5 = (f32[2,2048]{1,0:T(2,128)S(1)}, f32[2,2048]{1,0:T(2,128)S(1)}, u32[]{:S(2)}, u32[]{:S(2)}) collective-permute-start(f32[2,2048]{1,0:T(2,128)S(1)} %add.19), channel_id=1, source_target_pairs={{0,64},{64,0},{128,192},{192,128},{256,320},{320,256},{384,448},{4... | collective-permute-start | bytes 49160 | tf_op jit(solution)/shard_map/differences_over_replicas/ppermute | solution.py:213
  48.0 7.4 %collective-permute-start.6 = (f32[2,2048]{1,0:T(2,128)S(1)}, f32[2,2048]{1,0:T(2,128)S(1)}, u32[]{:S(2)}, u32[]{:S(2)}) collective-permute-start(f32[2,2048]{1,0:T(2,128)S(1)} %add.20), channel_id=1, source_target_pairs={{0,512},{64,576},{128,640},{192,704},{256,768},{320,832},{384,896}... | collective-permute-start | bytes 49160 | tf_op jit(solution)/shard_map/differences_over_replicas/ppermute | solution.py:213
  52.9 12.6 %collective-permute-start.4 = (s16[272,512]{1,0:T(8,128)(2,1)S(1)}, s16[272,512]{1,0:T(8,128)(2,1)S(1)}, u32[]{:S(2)}, u32[]{:S(2)}) collective-permute-start(s16[272,512]{1,0:T(8,128)(2,1)S(1)} %get-tuple-element.24), channel_id=1, source_target_pairs={{0,1},{1,0},{2,3},{3,2},{4,5},{5,4},{6,7},{7,6},{8,9},{9,8},{10,11... | collective-permute-start | bytes 835592 | tf_op jit(solution)/shard_map/along_line_first/ppermute | solution.py:237
  56.5 23.5 %collective-permute-start.8 = (s16[272,512]{1,0:T(8,128)(2,1)S(1)}, s16[272,512]{1,0:T(8,128)(2,1)S(1)}, u32[]{:S(2)}, u32[]{:S(2)}) collective-permute-start(s16[272,512]{1,0:T(8,128)(2,1)S(1)} %get-tuple-element.29), channel_id=1, source_target_pairs={{0,24},{1,25},{2,26},{3,27},{4,28},{5,29},{6,30},{7,31},{8,32},{9,... | collective-permute-start | bytes 835592 | tf_op jit(solution)/shard_map/far_along_ring/ppermute | solution.py:234
  62.3 24.8 %collective-permute-start.9 = (s16[272,512]{1,0:T(8,128)(2,1)S(1)}, s16[272,512]{1,0:T(8,128)(2,1)S(1)}, u32[]{:S(2)}, u32[]{:S(2)}) collective-permute-start(s16[272,512]{1,0:T(8,128)(2,1)S(1)} %get-tuple-element.30), channel_id=1, source_target_pairs={{0,40},{1,41},{2,42},{3,43},{4,44},{5,45},{6,46},{7,47},{8,48},{9,... | collective-permute-start | bytes 835592 | tf_op jit(solution)/shard_map/far_along_ring/ppermute | solution.py:234
  87.9 11.6 %collective-permute-start.10 = (s16[144,512]{1,0:T(8,128)(2,1)S(1)}, s16[144,512]{1,0:T(8,128)(2,1)S(1)}, u32[]{:S(2)}, u32[]{:S(2)}) collective-permute-start(s16[144,512]{1,0:T(8,128)(2,1)S(1)} %get-tuple-element.32), channel_id=1, source_target_pairs={{0,2},{1,3},{2,0},{3,1},{4,6},{5,7},{6,4},{7,5},{8,10},{9,11},{10,... | collective-permute-start | bytes 442376 | tf_op jit(solution)/shard_map/along_line/ppermute | solution.py:237
  100.2 13.7 %collective-permute-start.11 = (s16[80,512]{1,0:T(8,128)(2,1)S(1)}, s16[80,512]{1,0:T(8,128)(2,1)S(1)}, u32[]{:S(2)}, u32[]{:S(2)}) collective-permute-start(s16[80,512]{1,0:T(8,128)(2,1)S(1)} %get-tuple-element.34), channel_id=1, source_target_pairs={{0,4},{1,5},{2,6},{3,7},{4,0},{5,1},{6,2},{7,3},{8,12},{9,13},{10,... | collective-permute-start | bytes 245768 | tf_op jit(solution)/shard_map/along_line/ppermute | solution.py:237

commit v3 on v2

--- a/solution.py
+++ b/solution.py
@@ -12,6 +12,7 @@
 momentum_keep = 0.9
 ring, line = 8, 8
 group = 64
+shared = 128
 tail = 16
 steps_per_octave = 8.0
 top = 32760.0
@@ -79,22 +80,26 @@
 
 def pack_kernel(place, next_up, next_down, up, down, across, cotangent, above, below):
     width = up.shape[1]
-    half = width // 2
-    above[:, :width] = next_up[...]
-    below[:, :width] = next_down[...]
-    above[:, width:2 * width] = down[...]
-    below[:, width:2 * width] = up[...]
-    above[:, 2 * width:2 * width + half] = across[:, :half]
-    below[:, 2 * width:2 * width + half] = across[:, half:]
-    above[:, 2 * width + half:] = cotangent[...]
-    below[:, 2 * width + half:] = cotangent[...]
+    for message, near, far, rest in (
+        (above, next_up, down, across[:, :shared]),
+        (below, next_down, up, across[:, shared:]),
+    ):
+        keys = 2 * width + rest.shape[1]
+        message[:, :width] = near[...]
+        message[:, width:2 * width] = far[...]
+        message[:, 2 * width:keys] = rest
+        message[:, keys:] = cotangent[...]
 
 
 def pack(place, activations, cotangent):
-    columns = activations.shape[1] // ring * 5 // 2 + cotangent.shape[1]
-    out = jax.ShapeDtypeStruct((activations.shape[0], columns), activations.dtype)
+    tokens, width = activations.shape[0], activations.shape[1] // ring
+    columns = 2 * width + cotangent.shape[1]
+    outs = [
+        jax.ShapeDtypeStruct((tokens, columns + shared), activations.dtype),
+        jax.ShapeDtypeStruct((tokens, columns + width - shared), activations.dtype),
+    ]
     inputs = [(activations, shift) for shift in (1, -1, 2, -2, 4)] + [cotangent]
-    return on_chunks(pack_kernel, place, inputs, [out, out], mebibytes=60)
+    return on_chunks(pack_kernel, place, inputs, outs)
 
 
 def part(source, total, side, kept, sent):
@@ -107,13 +112,11 @@
 def sums_kernel(place, own, own_up, own_down, cotangent, below, above, far_sent, far_kept, near_sent, near_kept,
                 far, near, far_parted, near_parted):
     width = own.shape[1]
-    half = width // 2
-    keys = 2 * width + half
-    mine, under, over = cotangent[...], below[:, keys:], above[:, keys:]
+    mine, under, over = cotangent[...], below[:, 2 * width + shared:], above[:, 3 * width - shared:]
     far[:width] = product(own_up[...], mine) + product(above[:, width:2 * width], over)
-    far[:half] += product(below[:, 2 * width:keys], under)
+    far[:shared] += product(below[:, 2 * width:2 * width + shared], under)
     far[width:] = product(own_down[...], mine) + product(below[:, width:2 * width], under)
-    far[width + half:] += product(above[:, 2 * width:keys], over)
+    far[width + shared:] += product(above[:, 2 * width:3 * width - shared], over)
     part(far, far_parted, place[1], far_kept, far_sent)
     near[...] = product(own[...], mine) + product(below[:, :width], under) + product(above[:, :width], over)
     part(near, near_parted, place[1], near_kept, near_sent)
@@ -240,12 +243,12 @@
         above, below = pack(place, inputs, cotangent)
         received = [ring_move(above, 1), ring_move(below, -1)]
     picks, total, add_over = outer_sums(local, anchor, layer_fragment)
-    total = add_over(add_over(after(total, above), 2), 4)
+    total = add_over(add_over(after(total, above), 2), 8)
     sent, kept, near, here = sums(after(place, total), inputs, cotangent, *received)
     with jax.named_scope("along_line_first"):
         arrived = line_move(sent, 1)
         messages = [line_move(near, 1)]
-    total = add_over(add_over(after(total, sent), 1), 8)
+    total = add_over(add_over(after(total, sent), 1), 4)
     up, down = rest(after(place, total), kept, arrived)
     with jax.named_scope("far_along_ring"):
         messages += [ring_move(up, 3), ring_move(down, -3)]

time: 116 us -> 116 us (level)
  local copies, waits for them, and re-layouts: 0.05 us -> 2.58 us
  Pallas kernels: 10.8 us -> 9.21 us
    unnamed x14 -> x16, local copies, waits for them, and re-layouts: 0.03 us -> 2.57 us
    pallas_call x2, Pallas kernels: 7.06 us -> 5.44 us  [on_chunks(): pl.pallas_call(kernel, out_shape=outs, grid_spec=pltpu.PrefetchScalarGrid...]
  transfers between devices with their start and end apart: 12 -> 12, of which waited for: 7 -> 8; matrix products, arithmetic and copies ran while one was open for 1% -> 1% of each run, Pallas kernels for 1% -> 1%
where the time goes in v3:
time: 116 us; the launch traced here: 115 us
  starting transfers between devices  61.1 us (53%)
  waiting for transfers between devices  40.3 us (35%)
  Pallas kernels  9.21 us (8%)
  local copies, waits for them, and re-layouts  2.58 us (2%)
  other arithmetic  1.19 us (1%)
    ppermute x4, starting transfers between devices, add_over(): lax.ppermute(total, 'rep', [(r, r ^ bit) for r in range(groups)])  29.6 us
    ppermute x4, waiting for transfers between devices, ring_move(): return lax.ppermute(a, 'fsdp', along_ring(shift))  20.8 us
    ppermute x4, starting transfers between devices, line_move(): return lax.ppermute(a, 'fsdp', along_line(bit))  16.8 us
    ppermute x4, starting transfers between devices, ring_move(): return lax.ppermute(a, 'fsdp', along_ring(shift))  14.7 us
    ppermute x4, waiting for transfers between devices, line_move(): return lax.ppermute(a, 'fsdp', along_line(bit))  14.5 us
    pallas_call x2, Pallas kernels, on_chunks(): pl.pallas_call(kernel, out_shape=outs, grid_spec=pltpu.PrefetchScalarGrid...  5.44 us
    ppermute x4, waiting for transfers between devices, add_over(): lax.ppermute(total, 'rep', [(r, r ^ bit) for r in range(groups)])  5.06 us
    pallas_call x4, Pallas kernels, call(): pl.pallas_call(kernel, out_shape=[jax.ShapeDtypeStruct(s, d) for s, d in...  3.77 us
  transfers between devices with their start and end apart: 12, of which 8 were waited for; matrix products, arithmetic and copies ran while one was open for 1% of the time, Pallas kernels for 1%

profile of v3, /device:TPU:16, one launch (start us, length us, event | category | flops | bytes accessed | tf_op | source)
XLA Modules:
  0.0 115.3 jit_solution(16461128801502049555)
XLA Ops:
  0.7 0.1 pad_add_fusion.place
  0.7 0.0 copy-start
  0.7 1.6 %copy-done = bf16[1,256,4096]{2,1,0:T(8,128)(2,1)S(1)} copy-done((bf16[1,256,4096]{2,1,0:T(8,128)(2,1)S(1)}, bf16[1,256,4096]{2,1,0:T(8,128)(2,1)}, u32[]{:S(2)}) %copy-start) | copy-done | bytes 2097176
  2.3 0.0 copy-start.2
  2.3 0.9 copy-done.2
  3.3 0.0 copy-start.7
  3.3 0.0 copy-start.4
  3.3 0.0 copy-start.6
  3.3 0.0 copy-start.1
  3.3 0.0 copy-start.3
  3.3 2.0 %inputs_to_neighbours.1 = (bf16[256,1664]{1,0:T(8,128)(2,1)}, bf16[256,1920]{1,0:T(8,128)(2,1)}) custom-call(s32[4]{0:T(128)S(1)} %pad_add_fusion.place, bf16[256,4096]{1,0:T(8,128)(2,1)S(1)} %bitcast.25, bf16[256,4096]{1,0:T(8,128)(2,1)S(1)} %bitcast.26, bf16[256,4096]{1,0:T(8,128)(2,1)S(1)} %bitcast.27, bf16[256,4096]{1,0:T(8,128)(2,1)S(1)} %bitcast.28, ...), custom_call_target="tpu_custom_call" | custom-call | bytes 3000000 | tf_op jit(solution)/shard_map/inputs_to_neighbours/pallas_call | solution.py:66
  5.3 2.3 %collective-permute-start.3 = (bf16[256,1920]{1,0:T(8,128)(2,1)}, bf16[256,1920]{1,0:T(8,128)(2,1)S(1)}, u32[]{:S(2)}, u32[]{:S(2)}) collective-permute-start(bf16[256,1920]{1,0:T(8,128)(2,1)} %get-tuple-element.22), channel_id=1, source_target_pairs={{0,56},{1,57},{2,58},{3,59},{4,60},{5,61},{6,62},{7,63},{8,0},{9,1... | collective-permute-start | bytes 2949128 | tf_op jit(solution)/shard_map/inputs_to_neighbours/ppermute | solution.py:237
  7.6 3.5 %collective-permute-start.2 = (bf16[256,1664]{1,0:T(8,128)(2,1)}, bf16[256,1664]{1,0:T(8,128)(2,1)}, u32[]{:S(2)}, u32[]{:S(2)}) collective-permute-start(bf16[256,1664]{1,0:T(8,128)(2,1)} %get-tuple-element.19), channel_id=1, source_target_pairs={{0,8},{1,9},{2,10},{3,11},{4,12},{5,13},{6,14},{7,15},{8,16},{9,17... | collective-permute-start | bytes 2555912 | tf_op jit(solution)/shard_map/inputs_to_neighbours/ppermute | solution.py:237
  11.1 0.0 copy-done.7
  11.1 0.2 reduce-window.9
  11.3 0.0 copy-done.4
  11.3 0.0 copy-done.6
  11.3 0.1 select_reduce_fusion.1
  11.5 19.4 %collective-permute-start = (f32[2,2048]{1,0:T(2,128)S(1)}, f32[2,2048]{1,0:T(2,128)S(1)}, u32[]{:S(2)}, u32[]{:S(2)}) collective-permute-start(f32[2,2048]{1,0:T(2,128)S(1)} %pad_maximum_fusion), channel_id=1, source_target_pairs={{0,128},{64,192},{128,0},{192,64},{256,384},{320,448},{384,256},{4... | collective-permute-start | bytes 49160 | tf_op jit(solution)/shard_map/differences_over_replicas/ppermute | solution.py:216
  30.8 1.7 %collective-permute-done = f32[2,2048]{1,0:T(2,128)S(1)} collective-permute-done((f32[2,2048]{1,0:T(2,128)S(1)}, f32[2,2048]{1,0:T(2,128)S(1)}, u32[]{:S(2)}, u32[]{:S(2)}) %collective-permute-start) | collective-permute-done | bytes 16416 | tf_op jit(solution)/shard_map/differences_over_replicas/ppermute | solution.py:216
  32.6 4.9 %collective-permute-start.1 = (f32[2,2048]{1,0:T(2,128)S(1)}, f32[2,2048]{1,0:T(2,128)S(1)}, u32[]{:S(2)}, u32[]{:S(2)}) collective-permute-start(f32[2,2048]{1,0:T(2,128)S(1)} %add.18), channel_id=1, source_target_pairs={{0,512},{64,576},{128,640},{192,704},{256,768},{320,832},{384,896}... | collective-permute-start | bytes 49160 | tf_op jit(solution)/shard_map/differences_over_replicas/ppermute | solution.py:216
  37.5 2.2 %collective-permute-done.1 = f32[2,2048]{1,0:T(2,128)S(1)} collective-permute-done((f32[2,2048]{1,0:T(2,128)S(1)}, f32[2,2048]{1,0:T(2,128)S(1)}, u32[]{:S(2)}, u32[]{:S(2)}) %collective-permute-start.1) | collective-permute-done | bytes 16416 | tf_op jit(solution)/shard_map/differences_over_replicas/ppermute | solution.py:216
  39.7 0.0 collective-permute-done.2.below
  39.7 0.0 collective-permute-done.3.above
  39.7 0.0 copy-done.1
  39.7 0.0 copy-done.3
  39.8 3.5 %shard_map.85 = (s16[528,512]{1,0:T(8,128)(2,1)S(1)}, f32[512,512]{1,0:T(8,128)S(1)}, s16[272,512]{1,0:T(8,128)(2,1)S(1)}, f32[256,512]{1,0:T(8,128)S(1)}) custom-call(s32[4]{0:T(128)S(1)} %pad_add_fusion.place, bf16[256,4096]{1,0:T(8,128)(2,1)S(1)} %bitcast.30, bf16[256,4096]{1,0:T(8,128)(2,1)S(1)} %bitcast.31, bf16[256,4096]{1,0:T(8,128)(2,1)S(1)} %bitcast.32, ...), custom_call_target="tpu_custom_call" | custom-call | bytes 3000000 | tf_op jit(solution)/shard_map/pallas_call | solution.py:66
  43.2 0.0 copy-start.5
  43.3 3.5 %collective-permute-start.7 = (s16[528,512]{1,0:T(8,128)(2,1)S(1)}, s16[528,512]{1,0:T(8,128)(2,1)S(1)}, u32[]{:S(2)}, u32[]{:S(2)}) collective-permute-start(s16[528,512]{1,0:T(8,128)(2,1)S(1)} %get-tuple-element.25), channel_id=1, source_target_pairs={{0,1},{1,0},{2,3},{3,2},{4,5},{5,4},{6,7},{7,6},{8,9},{9,8},{10,11... | collective-permute-start | bytes 1622024 | tf_op jit(solution)/shard_map/along_line_first/ppermute | solution.py:240
  46.8 1.9 %collective-permute-start.5 = (f32[2,2048]{1,0:T(2,128)S(1)}, f32[2,2048]{1,0:T(2,128)S(1)}, u32[]{:S(2)}, u32[]{:S(2)}) collective-permute-start(f32[2,2048]{1,0:T(2,128)S(1)} %add.19), channel_id=1, source_target_pairs={{0,64},{64,0},{128,192},{192,128},{256,320},{320,256},{384,448},{4... | collective-permute-start | bytes 49160 | tf_op jit(solution)/shard_map/differences_over_replicas/ppermute | solution.py:216
  48.7 1.1 collective-permute-done.5
  49.9 3.4 %collective-permute-start.6 = (f32[2,2048]{1,0:T(2,128)S(1)}, f32[2,2048]{1,0:T(2,128)S(1)}, u32[]{:S(2)}, u32[]{:S(2)}) collective-permute-start(f32[2,2048]{1,0:T(2,128)S(1)} %add.20), channel_id=1, source_target_pairs={{0,256},{64,320},{128,384},{192,448},{256,0},{320,64},{384,128},{4... | collective-permute-start | bytes 49160 | tf_op jit(solution)/shard_map/differences_over_replicas/ppermute | solution.py:216
  53.3 2.5 %collective-permute-start.4 = (s16[272,512]{1,0:T(8,128)(2,1)S(1)}, s16[272,512]{1,0:T(8,128)(2,1)S(1)}, u32[]{:S(2)}, u32[]{:S(2)}) collective-permute-start(s16[272,512]{1,0:T(8,128)(2,1)S(1)} %get-tuple-element.24), channel_id=1, source_target_pairs={{0,1},{1,0},{2,3},{3,2},{4,5},{5,4},{6,7},{7,6},{8,9},{9,8},{10,11... | collective-permute-start | bytes 835592 | tf_op jit(solution)/shard_map/along_line_first/ppermute | solution.py:240
  55.8 0.0 collective-permute-done.6
  55.8 0.9 collective-permute-done.7.message
  56.7 1.0 shard_map.86
  57.7 5.8 %collective-permute-start.8 = (s16[272,512]{1,0:T(8,128)(2,1)S(1)}, s16[272,512]{1,0:T(8,128)(2,1)S(1)}, u32[]{:S(2)}, u32[]{:S(2)}) collective-permute-start(s16[272,512]{1,0:T(8,128)(2,1)S(1)} %get-tuple-element.29), channel_id=1, source_target_pairs={{0,24},{1,25},{2,26},{3,27},{4,28},{5,29},{6,30},{7,31},{8,32},{9,... | collective-permute-start | bytes 835592 | tf_op jit(solution)/shard_map/far_along_ring/ppermute | solution.py:237
  63.6 3.0 %collective-permute-start.9 = (s16[272,512]{1,0:T(8,128)(2,1)S(1)}, s16[272,512]{1,0:T(8,128)(2,1)S(1)}, u32[]{:S(2)}, u32[]{:S(2)}) collective-permute-start(s16[272,512]{1,0:T(8,128)(2,1)S(1)} %get-tuple-element.30), channel_id=1, source_target_pairs={{0,40},{1,41},{2,42},{3,43},{4,44},{5,45},{6,46},{7,47},{8,48},{9,... | collective-permute-start | bytes 835592 | tf_op jit(solution)/shard_map/far_along_ring/ppermute | solution.py:237
  66.6 0.0 collective-permute-done.4.refs_0_
  66.6 14.3 %collective-permute-done.8.refs_1_ = s16[272,512]{1,0:T(8,128)(2,1)S(1)} collective-permute-done((s16[272,512]{1,0:T(8,128)(2,1)S(1)}, s16[272,512]{1,0:T(8,128)(2,1)S(1)}, u32[]{:S(2)}, u32[]{:S(2)}) %collective-permute-start.8) | collective-permute-done | bytes 278560 | tf_op jit(solution)/shard_map/far_along_ring/ppermute | solution.py:237
  80.9 6.5 %collective-permute-done.9.refs_2_ = s16[272,512]{1,0:T(8,128)(2,1)S(1)} collective-permute-done((s16[272,512]{1,0:T(8,128)(2,1)S(1)}, s16[272,512]{1,0:T(8,128)(2,1)S(1)}, u32[]{:S(2)}, u32[]{:S(2)}) %collective-permute-start.9) | collective-permute-done | bytes 278560 | tf_op jit(solution)/shard_map/far_along_ring/ppermute | solution.py:237
  87.4 0.9 along_line.2
  88.3 4.4 %collective-permute-start.10 = (s16[144,512]{1,0:T(8,128)(2,1)S(1)}, s16[144,512]{1,0:T(8,128)(2,1)S(1)}, u32[]{:S(2)}, u32[]{:S(2)}) collective-permute-start(s16[144,512]{1,0:T(8,128)(2,1)S(1)} %get-tuple-element.32), channel_id=1, source_target_pairs={{0,2},{1,3},{2,0},{3,1},{4,6},{5,7},{6,4},{7,5},{8,10},{9,11},{10,... | collective-permute-start | bytes 442376 | tf_op jit(solution)/shard_map/along_line/ppermute | solution.py:240
  92.7 7.1 %collective-permute-done.10.refs_0_ = s16[144,512]{1,0:T(8,128)(2,1)S(1)} collective-permute-done((s16[144,512]{1,0:T(8,128)(2,1)S(1)}, s16[144,512]{1,0:T(8,128)(2,1)S(1)}, u32[]{:S(2)}, u32[]{:S(2)}) %collective-permute-start.10) | collective-permute-done | bytes 147488 | tf_op jit(solution)/shard_map/along_line/ppermute | solution.py:240
  99.8 0.6 along_line.3
  100.5 6.4 %collective-permute-start.11 = (s16[80,512]{1,0:T(8,128)(2,1)S(1)}, s16[80,512]{1,0:T(8,128)(2,1)S(1)}, u32[]{:S(2)}, u32[]{:S(2)}) collective-permute-start(s16[80,512]{1,0:T(8,128)(2,1)S(1)} %get-tuple-element.34), channel_id=1, source_target_pairs={{0,4},{1,5},{2,6},{3,7},{4,0},{5,1},{6,2},{7,3},{8,12},{9,13},{10,... | collective-permute-start | bytes 245768 | tf_op jit(solution)/shard_map/along_line/ppermute | solution.py:240
  106.9 0.0 copy-done.5
  106.9 0.7 fusion.1
  107.6 6.5 %collective-permute-done.11.message = s16[80,512]{1,0:T(8,128)(2,1)S(1)} collective-permute-done((s16[80,512]{1,0:T(8,128)(2,1)S(1)}, s16[80,512]{1,0:T(8,128)(2,1)S(1)}, u32[]{:S(2)}, u32[]{:S(2)}) %collective-permute-start.11) | collective-permute-done | bytes 81952 | tf_op jit(solution)/shard_map/along_line/ppermute | solution.py:240
  114.1 1.2 %shard_map.87 = f32[64,512]{1,0:T(8,128)} custom-call(s32[4]{0:T(128)S(1)} %pad_add_fusion.place, f32[64,512]{1,0:T(8,128)S(1)} %get-tuple-element.33.kept, s16[80,512]{1,0:T(8,128)(2,1)S(1)} %collective-permute-done.11.message), custom_call_target="tpu_custom_call" | custom-call | bytes 3000000 | tf_op jit(solution)/shard_map/pallas_call | solution.py:141
  (8 shorter events, 0.1 us)
Async XLA Ops:
  0.7 1.6 %copy-start = (bf16[1,256,4096]{2,1,0:T(8,128)(2,1)S(1)}, bf16[1,256,4096]{2,1,0:T(8,128)(2,1)}, u32[]{:S(2)}) copy-start(bf16[1,256,4096]{2,1,0:T(8,128)(2,1)} %param.6) | copy-start | bytes 6291460
  2.3 0.9 copy-start.2
  3.3 7.8 %copy-start.7 = (s32[8]{0:T(128)S(1)}, s32[8]{0:T(128)}, u32[]{:S(2)}) copy-start(s32[8]{0:T(128)} %param.11) | copy-start | bytes 100
  3.3 8.0 %copy-start.4 = (f32[8,2048]{1,0:T(8,128)S(1)}, f32[8,2048]{1,0:T(8,128)}, u32[]{:S(2)}) copy-start(f32[8,2048]{1,0:T(8,128)} %param.9) | copy-start | bytes 196612
  3.3 8.0 %copy-start.6 = (f32[1,8,2048]{2,1,0:T(8,128)S(1)}, f32[1,8,2048]{2,1,0:T(8,128)}, u32[]{:S(2)}) copy-start(f32[1,8,2048]{2,1,0:T(8,128)} %param.8) | copy-start | bytes 196612
  3.3 36.5 %copy-start.1 = (bf16[1,256,4096]{2,1,0:T(8,128)(2,1)S(1)}, bf16[1,256,4096]{2,1,0:T(8,128)(2,1)}, u32[]{:S(2)}) copy-start(bf16[1,256,4096]{2,1,0:T(8,128)(2,1)} %param.6) | copy-start | bytes 6291460
  3.3 36.5 %copy-start.3 = (bf16[1,256,512]{2,1,0:T(8,128)(2,1)S(1)}, bf16[1,256,512]{2,1,0:T(8,128)(2,1)}, u32[]{:S(2)}) copy-start(bf16[1,256,512]{2,1,0:T(8,128)(2,1)} %param.7) | copy-start | bytes 786436
  5.3 34.5 %collective-permute-start.3 = (bf16[256,1920]{1,0:T(8,128)(2,1)}, bf16[256,1920]{1,0:T(8,128)(2,1)S(1)}, u32[]{:S(2)}, u32[]{:S(2)}) collective-permute-start(bf16[256,1920]{1,0:T(8,128)(2,1)} %get-tuple-element.22), channel_id=1, source_target_pairs={{0,56},{1,57},{2,58},{3,59},{4,60},{5,61},{6,62},{7,63},{8,0},{9,1... | collective-permute-start | bytes 2949128 | tf_op jit(solution)/shard_map/inputs_to_neighbours/ppermute | solution.py:237
  7.6 32.1 %collective-permute-start.2 = (bf16[256,1664]{1,0:T(8,128)(2,1)}, bf16[256,1664]{1,0:T(8,128)(2,1)}, u32[]{:S(2)}, u32[]{:S(2)}) collective-permute-start(bf16[256,1664]{1,0:T(8,128)(2,1)} %get-tuple-element.19), channel_id=1, source_target_pairs={{0,8},{1,9},{2,10},{3,11},{4,12},{5,13},{6,14},{7,15},{8,16},{9,17... | collective-permute-start | bytes 2555912 | tf_op jit(solution)/shard_map/inputs_to_neighbours/ppermute | solution.py:237
  11.5 21.1 %collective-permute-start = (f32[2,2048]{1,0:T(2,128)S(1)}, f32[2,2048]{1,0:T(2,128)S(1)}, u32[]{:S(2)}, u32[]{:S(2)}) collective-permute-start(f32[2,2048]{1,0:T(2,128)S(1)} %pad_maximum_fusion), channel_id=1, source_target_pairs={{0,128},{64,192},{128,0},{192,64},{256,384},{320,448},{384,256},{4... | collective-permute-start | bytes 49160 | tf_op jit(solution)/shard_map/differences_over_replicas/ppermute | solution.py:216
  32.6 7.1 %collective-permute-start.1 = (f32[2,2048]{1,0:T(2,128)S(1)}, f32[2,2048]{1,0:T(2,128)S(1)}, u32[]{:S(2)}, u32[]{:S(2)}) collective-permute-start(f32[2,2048]{1,0:T(2,128)S(1)} %add.18), channel_id=1, source_target_pairs={{0,512},{64,576},{128,640},{192,704},{256,768},{320,832},{384,896}... | collective-permute-start | bytes 49160 | tf_op jit(solution)/shard_map/differences_over_replicas/ppermute | solution.py:216
  43.2 63.6 %copy-start.5 = (f32[8,2048]{1,0:T(8,128)S(1)}, f32[8,2048]{1,0:T(8,128)}, u32[]{:S(2)}) copy-start(f32[8,2048]{1,0:T(8,128)} %param.10) | copy-start | bytes 196612
  43.3 13.5 %collective-permute-start.7 = (s16[528,512]{1,0:T(8,128)(2,1)S(1)}, s16[528,512]{1,0:T(8,128)(2,1)S(1)}, u32[]{:S(2)}, u32[]{:S(2)}) collective-permute-start(s16[528,512]{1,0:T(8,128)(2,1)S(1)} %get-tuple-element.25), channel_id=1, source_target_pairs={{0,1},{1,0},{2,3},{3,2},{4,5},{5,4},{6,7},{7,6},{8,9},{9,8},{10,11... | collective-permute-start | bytes 1622024 | tf_op jit(solution)/shard_map/along_line_first/ppermute | solution.py:240
  46.8 3.1 %collective-permute-start.5 = (f32[2,2048]{1,0:T(2,128)S(1)}, f32[2,2048]{1,0:T(2,128)S(1)}, u32[]{:S(2)}, u32[]{:S(2)}) collective-permute-start(f32[2,2048]{1,0:T(2,128)S(1)} %add.19), channel_id=1, source_target_pairs={{0,64},{64,0},{128,192},{192,128},{256,320},{320,256},{384,448},{4... | collective-permute-start | bytes 49160 | tf_op jit(solution)/shard_map/differences_over_replicas/ppermute | solution.py:216
  49.9 5.9 %collective-permute-start.6 = (f32[2,2048]{1,0:T(2,128)S(1)}, f32[2,2048]{1,0:T(2,128)S(1)}, u32[]{:S(2)}, u32[]{:S(2)}) collective-permute-start(f32[2,2048]{1,0:T(2,128)S(1)} %add.20), channel_id=1, source_target_pairs={{0,256},{64,320},{128,384},{192,448},{256,0},{320,64},{384,128},{4... | collective-permute-start | bytes 49160 | tf_op jit(solution)/shard_map/differences_over_replicas/ppermute | solution.py:216
  53.3 13.3 %collective-permute-start.4 = (s16[272,512]{1,0:T(8,128)(2,1)S(1)}, s16[272,512]{1,0:T(8,128)(2,1)S(1)}, u32[]{:S(2)}, u32[]{:S(2)}) collective-permute-start(s16[272,512]{1,0:T(8,128)(2,1)S(1)} %get-tuple-element.24), channel_id=1, source_target_pairs={{0,1},{1,0},{2,3},{3,2},{4,5},{5,4},{6,7},{7,6},{8,9},{9,8},{10,11... | collective-permute-start | bytes 835592 | tf_op jit(solution)/shard_map/along_line_first/ppermute | solution.py:240
  57.7 23.2 %collective-permute-start.8 = (s16[272,512]{1,0:T(8,128)(2,1)S(1)}, s16[272,512]{1,0:T(8,128)(2,1)S(1)}, u32[]{:S(2)}, u32[]{:S(2)}) collective-permute-start(s16[272,512]{1,0:T(8,128)(2,1)S(1)} %get-tuple-element.29), channel_id=1, source_target_pairs={{0,24},{1,25},{2,26},{3,27},{4,28},{5,29},{6,30},{7,31},{8,32},{9,... | collective-permute-start | bytes 835592 | tf_op jit(solution)/shard_map/far_along_ring/ppermute | solution.py:237
  63.6 23.8 %collective-permute-start.9 = (s16[272,512]{1,0:T(8,128)(2,1)S(1)}, s16[272,512]{1,0:T(8,128)(2,1)S(1)}, u32[]{:S(2)}, u32[]{:S(2)}) collective-permute-start(s16[272,512]{1,0:T(8,128)(2,1)S(1)} %get-tuple-element.30), channel_id=1, source_target_pairs={{0,40},{1,41},{2,42},{3,43},{4,44},{5,45},{6,46},{7,47},{8,48},{9,... | collective-permute-start | bytes 835592 | tf_op jit(solution)/shard_map/far_along_ring/ppermute | solution.py:237
  88.3 11.5 %collective-permute-start.10 = (s16[144,512]{1,0:T(8,128)(2,1)S(1)}, s16[144,512]{1,0:T(8,128)(2,1)S(1)}, u32[]{:S(2)}, u32[]{:S(2)}) collective-permute-start(s16[144,512]{1,0:T(8,128)(2,1)S(1)} %get-tuple-element.32), channel_id=1, source_target_pairs={{0,2},{1,3},{2,0},{3,1},{4,6},{5,7},{6,4},{7,5},{8,10},{9,11},{10,... | collective-permute-start | bytes 442376 | tf_op jit(solution)/shard_map/along_line/ppermute | solution.py:240
  100.5 13.6 %collective-permute-start.11 = (s16[80,512]{1,0:T(8,128)(2,1)S(1)}, s16[80,512]{1,0:T(8,128)(2,1)S(1)}, u32[]{:S(2)}, u32[]{:S(2)}) collective-permute-start(s16[80,512]{1,0:T(8,128)(2,1)S(1)} %get-tuple-element.34), channel_id=1, source_target_pairs={{0,4},{1,5},{2,6},{3,7},{4,0},{5,1},{6,2},{7,3},{8,12},{9,13},{10,... | collective-permute-start | bytes 245768 | tf_op jit(solution)/shard_map/along_line/ppermute | solution.py:240

commit v4 on v3

--- a/solution.py
+++ b/solution.py
@@ -78,28 +78,49 @@
     )(place, *[a[0] if isinstance(a, tuple) else a for a in inputs])
 
 
-def pack_kernel(place, next_up, next_down, up, down, across, cotangent, above, below):
-    width = up.shape[1]
-    for message, near, far, rest in (
-        (above, next_up, down, across[:, :shared]),
-        (below, next_down, up, across[:, shared:]),
-    ):
-        keys = 2 * width + rest.shape[1]
-        message[:, :width] = near[...]
-        message[:, width:2 * width] = far[...]
-        message[:, 2 * width:keys] = rest
-        message[:, keys:] = cotangent[...]
-
-
-def pack(place, activations, cotangent):
+def pack_kernel(activations, cotangent, above, below, sems):
+    width = activations.shape[1] // ring
+    y = lax.div(lax.axis_index("fsdp"), line)
+
+    def chunk(shift, start=0, size=width):
+        at = lax.rem(y + shift + ring, ring) * width + start
+        return activations.at[:, pl.ds(pl.multiple_of(at, 128), size)]
+
+    rest = width - shared
+    pieces = [
+        (chunk(-1), below, 0),
+        (chunk(1), above, 0),
+        (chunk(2), below, width),
+        (chunk(-2), above, width),
+        (chunk(4, shared, rest), below, 2 * width),
+        (chunk(4, 0, shared), above, 2 * width),
+        (cotangent, below, 2 * width + rest),
+        (cotangent, above, 2 * width + shared),
+    ]
+    copies = [
+        pltpu.make_async_copy(piece, message.at[:, pl.ds(start, piece.shape[1])], sems.at[i])
+        for i, (piece, message, start) in enumerate(pieces)
+    ]
+    for c in copies:
+        c.start()
+    for c in copies:
+        c.wait()
+
+
+def pack(activations, cotangent):
     tokens, width = activations.shape[0], activations.shape[1] // ring
     columns = 2 * width + cotangent.shape[1]
-    outs = [
-        jax.ShapeDtypeStruct((tokens, columns + shared), activations.dtype),
-        jax.ShapeDtypeStruct((tokens, columns + width - shared), activations.dtype),
-    ]
-    inputs = [(activations, shift) for shift in (1, -1, 2, -2, 4)] + [cotangent]
-    return on_chunks(pack_kernel, place, inputs, outs)
+    return pl.pallas_call(
+        pack_kernel,
+        out_shape=[
+            jax.ShapeDtypeStruct((tokens, columns + shared), activations.dtype),
+            jax.ShapeDtypeStruct((tokens, columns + width - shared), activations.dtype),
+        ],
+        in_specs=[anywhere, anywhere],
+        out_specs=[whole, whole],
+        scratch_shapes=[pltpu.SemaphoreType.DMA((8,))],
+        compiler_params=pltpu.CompilerParams(vmem_limit_bytes=60 * 1024 * 1024),
+    )(activations, cotangent)
 
 
 def part(source, total, side, kept, sent):
@@ -240,10 +261,10 @@
         return lax.ppermute(a, "fsdp", along_line(bit))
 
     with jax.named_scope("inputs_to_neighbours"):
-        above, below = pack(place, inputs, cotangent)
+        above, below = pack(inputs, cotangent)
         received = [ring_move(above, 1), ring_move(below, -1)]
     picks, total, add_over = outer_sums(local, anchor, layer_fragment)
-    total = add_over(add_over(after(total, above), 2), 8)
+    total = add_over(add_over(after(total, above), 8), 2)
     sent, kept, near, here = sums(after(place, total), inputs, cotangent, *received)
     with jax.named_scope("along_line_first"):
         arrived = line_move(sent, 1)

time: 116 us -> 115 us (level)
  local copies, waits for them, and re-layouts: 2.58 us -> 0.04 us
    pallas_call x0 -> x1, Pallas kernels: none -> 2.89 us  [pack(): pl.pallas_call(pack_kernel, out_shape=[jax.ShapeDtypeStruct((tokens, colu...]
    unnamed x16 -> x10, local copies, waits for them, and re-layouts: 2.57 us -> 0.03 us
    pallas_call x2 -> x1, Pallas kernels: 5.44 us -> 3.49 us  [on_chunks(): pl.pallas_call(kernel, out_shape=outs, grid_spec=pltpu.PrefetchScalarGrid...]
  transfers between devices with their start and end apart: 12 -> 12, of which waited for: 8 -> 8; matrix products, arithmetic and copies ran while one was open for 1% -> 2% of each run, Pallas kernels for 1% -> 1%
where the time goes in v4:
time: 115 us; the launch traced here: 114 us
  starting transfers between devices  61.1 us (53%)
  waiting for transfers between devices  40.2 us (35%)
  Pallas kernels  10.2 us (9%)
  other arithmetic  2.07 us (2%)
    ppermute x4, starting transfers between devices, add_over(): lax.ppermute(total, 'rep', [(r, r ^ bit) for r in range(groups)])  29.6 us
    ppermute x4, waiting for transfers between devices, ring_move(): return lax.ppermute(a, 'fsdp', along_ring(shift))  20.6 us
    ppermute x4, starting transfers between devices, line_move(): return lax.ppermute(a, 'fsdp', along_line(bit))  16.8 us
    ppermute x4, starting transfers between devices, ring_move(): return lax.ppermute(a, 'fsdp', along_ring(shift))  14.7 us
    ppermute x4, waiting for transfers between devices, line_move(): return lax.ppermute(a, 'fsdp', along_line(bit))  14.6 us
    ppermute x4, waiting for transfers between devices, add_over(): lax.ppermute(total, 'rep', [(r, r ^ bit) for r in range(groups)])  4.95 us
    pallas_call x4, Pallas kernels, call(): pl.pallas_call(kernel, out_shape=[jax.ShapeDtypeStruct(s, d) for s, d in...  3.78 us
    pallas_call x1, Pallas kernels, on_chunks(): pl.pallas_call(kernel, out_shape=outs, grid_spec=pltpu.PrefetchScalarGrid...  3.49 us
  transfers between devices with their start and end apart: 12, of which 8 were waited for; matrix products, arithmetic and copies ran while one was open for 2% of the time, Pallas kernels for 1%

profile of v4, /device:TPU:16, one launch (start us, length us, event | category | flops | bytes accessed | tf_op | source)
XLA Modules:
  0.0 114.5 jit_solution(15928335501640883251)
XLA Ops:
  0.6 0.0 copy-start.1
  0.6 0.0 copy-start
  0.7 0.0 copy-start.4
  0.7 2.9 %inputs_to_neighbours.1 = (bf16[256,1664]{1,0:T(8,128)(2,1)}, bf16[256,1920]{1,0:T(8,128)(2,1)}) custom-call(bf16[256,4096]{1,0:T(8,128)(2,1)} %bitcast.25, bf16[256,512]{1,0:T(8,128)(2,1)} %bitcast.29), custom_call_target="tpu_custom_call" | custom-call | tf_op jit(solution)/shard_map/inputs_to_neighbours/pallas_call | solution.py:113
  3.6 2.4 %collective-permute-start.3 = (bf16[256,1920]{1,0:T(8,128)(2,1)}, bf16[256,1920]{1,0:T(8,128)(2,1)S(1)}, u32[]{:S(2)}, u32[]{:S(2)}) collective-permute-start(bf16[256,1920]{1,0:T(8,128)(2,1)} %get-tuple-element.22), channel_id=1, source_target_pairs={{0,56},{1,57},{2,58},{3,59},{4,60},{5,61},{6,62},{7,63},{8,0},{9,1... | collective-permute-start | bytes 2949128 | tf_op jit(solution)/shard_map/inputs_to_neighbours/ppermute | solution.py:258
  5.9 3.5 %collective-permute-start.2 = (bf16[256,1664]{1,0:T(8,128)(2,1)}, bf16[256,1664]{1,0:T(8,128)(2,1)}, u32[]{:S(2)}, u32[]{:S(2)}) collective-permute-start(bf16[256,1664]{1,0:T(8,128)(2,1)} %get-tuple-element.19), channel_id=1, source_target_pairs={{0,8},{1,9},{2,10},{3,11},{4,12},{5,13},{6,14},{7,15},{8,16},{9,17... | collective-permute-start | bytes 2555912 | tf_op jit(solution)/shard_map/inputs_to_neighbours/ppermute | solution.py:258
  9.4 0.0 copy-done.4
  9.4 0.2 reduce-window.9
  9.6 1.0 select_reduce_fusion.1
  10.6 4.9 %collective-permute-start = (f32[2,2048]{1,0:T(2,128)S(1)}, f32[2,2048]{1,0:T(2,128)S(1)}, u32[]{:S(2)}, u32[]{:S(2)}) collective-permute-start(f32[2,2048]{1,0:T(2,128)S(1)} %pad_maximum_fusion), channel_id=1, source_target_pairs={{0,512},{64,576},{128,640},{192,704},{256,768},{320,832},{384,896}... | collective-permute-start | bytes 49160 | tf_op jit(solution)/shard_map/differences_over_replicas/ppermute | solution.py:237
  15.6 2.2 %collective-permute-done = f32[2,2048]{1,0:T(2,128)S(1)} collective-permute-done((f32[2,2048]{1,0:T(2,128)S(1)}, f32[2,2048]{1,0:T(2,128)S(1)}, u32[]{:S(2)}, u32[]{:S(2)}) %collective-permute-start) | collective-permute-done | bytes 16416 | tf_op jit(solution)/shard_map/differences_over_replicas/ppermute | solution.py:237
  17.8 19.4 %collective-permute-start.1 = (f32[2,2048]{1,0:T(2,128)S(1)}, f32[2,2048]{1,0:T(2,128)S(1)}, u32[]{:S(2)}, u32[]{:S(2)}) collective-permute-start(f32[2,2048]{1,0:T(2,128)S(1)} %add.18), channel_id=1, source_target_pairs={{0,128},{64,192},{128,0},{192,64},{256,384},{320,448},{384,256},{4... | collective-permute-start | bytes 49160 | tf_op jit(solution)/shard_map/differences_over_replicas/ppermute | solution.py:237
  37.2 0.1 pad_add_fusion.place
  37.2 1.6 %collective-permute-done.1 = f32[2,2048]{1,0:T(2,128)S(1)} collective-permute-done((f32[2,2048]{1,0:T(2,128)S(1)}, f32[2,2048]{1,0:T(2,128)S(1)}, u32[]{:S(2)}, u32[]{:S(2)}) %collective-permute-start.1) | collective-permute-done | bytes 16416 | tf_op jit(solution)/shard_map/differences_over_replicas/ppermute | solution.py:237
  38.9 0.0 collective-permute-done.2.below
  38.9 0.0 collective-permute-done.3.above
  38.9 0.0 copy-done.1
  38.9 0.0 copy-done
  38.9 3.5 %shard_map.85 = (s16[528,512]{1,0:T(8,128)(2,1)S(1)}, f32[512,512]{1,0:T(8,128)S(1)}, s16[272,512]{1,0:T(8,128)(2,1)S(1)}, f32[256,512]{1,0:T(8,128)S(1)}) custom-call(s32[4]{0:T(128)S(1)} %pad_add_fusion.place, bf16[256,4096]{1,0:T(8,128)(2,1)S(1)} %bitcast.26, bf16[256,4096]{1,0:T(8,128)(2,1)S(1)} %bitcast.27, bf16[256,4096]{1,0:T(8,128)(2,1)S(1)} %bitcast.28, ...), custom_call_target="tpu_custom_call" | custom-call | bytes 3000000 | tf_op jit(solution)/shard_map/pallas_call | solution.py:66
  42.4 0.0 copy-start.2
  42.4 0.0 copy-start.3
  42.5 3.5 %collective-permute-start.7 = (s16[528,512]{1,0:T(8,128)(2,1)S(1)}, s16[528,512]{1,0:T(8,128)(2,1)S(1)}, u32[]{:S(2)}, u32[]{:S(2)}) collective-permute-start(s16[528,512]{1,0:T(8,128)(2,1)S(1)} %get-tuple-element.25), channel_id=1, source_target_pairs={{0,1},{1,0},{2,3},{3,2},{4,5},{5,4},{6,7},{7,6},{8,9},{9,8},{10,11... | collective-permute-start | bytes 1622024 | tf_op jit(solution)/shard_map/along_line_first/ppermute | solution.py:261
  46.0 1.9 %collective-permute-start.5 = (f32[2,2048]{1,0:T(2,128)S(1)}, f32[2,2048]{1,0:T(2,128)S(1)}, u32[]{:S(2)}, u32[]{:S(2)}) collective-permute-start(f32[2,2048]{1,0:T(2,128)S(1)} %add.19), channel_id=1, source_target_pairs={{0,64},{64,0},{128,192},{192,128},{256,320},{320,256},{384,448},{4... | collective-permute-start | bytes 49160 | tf_op jit(solution)/shard_map/differences_over_replicas/ppermute | solution.py:237
  47.9 1.1 %collective-permute-done.5 = f32[2,2048]{1,0:T(2,128)S(1)} collective-permute-done((f32[2,2048]{1,0:T(2,128)S(1)}, f32[2,2048]{1,0:T(2,128)S(1)}, u32[]{:S(2)}, u32[]{:S(2)}) %collective-permute-start.5) | collective-permute-done | bytes 16416 | tf_op jit(solution)/shard_map/differences_over_replicas/ppermute | solution.py:237
  49.1 3.4 %collective-permute-start.6 = (f32[2,2048]{1,0:T(2,128)S(1)}, f32[2,2048]{1,0:T(2,128)S(1)}, u32[]{:S(2)}, u32[]{:S(2)}) collective-permute-start(f32[2,2048]{1,0:T(2,128)S(1)} %add.20), channel_id=1, source_target_pairs={{0,256},{64,320},{128,384},{192,448},{256,0},{320,64},{384,128},{4... | collective-permute-start | bytes 49160 | tf_op jit(solution)/shard_map/differences_over_replicas/ppermute | solution.py:237
  52.5 2.5 %collective-permute-start.4 = (s16[272,512]{1,0:T(8,128)(2,1)S(1)}, s16[272,512]{1,0:T(8,128)(2,1)S(1)}, u32[]{:S(2)}, u32[]{:S(2)}) collective-permute-start(s16[272,512]{1,0:T(8,128)(2,1)S(1)} %get-tuple-element.24), channel_id=1, source_target_pairs={{0,1},{1,0},{2,3},{3,2},{4,5},{5,4},{6,7},{7,6},{8,9},{9,8},{10,11... | collective-permute-start | bytes 835592 | tf_op jit(solution)/shard_map/along_line_first/ppermute | solution.py:261
  54.9 0.0 collective-permute-done.6
  55.0 1.1 collective-permute-done.7.message
  56.1 1.0 shard_map.86
  57.1 5.8 %collective-permute-start.8 = (s16[272,512]{1,0:T(8,128)(2,1)S(1)}, s16[272,512]{1,0:T(8,128)(2,1)S(1)}, u32[]{:S(2)}, u32[]{:S(2)}) collective-permute-start(s16[272,512]{1,0:T(8,128)(2,1)S(1)} %get-tuple-element.29), channel_id=1, source_target_pairs={{0,24},{1,25},{2,26},{3,27},{4,28},{5,29},{6,30},{7,31},{8,32},{9,... | collective-permute-start | bytes 835592 | tf_op jit(solution)/shard_map/far_along_ring/ppermute | solution.py:258
  62.9 3.0 %collective-permute-start.9 = (s16[272,512]{1,0:T(8,128)(2,1)S(1)}, s16[272,512]{1,0:T(8,128)(2,1)S(1)}, u32[]{:S(2)}, u32[]{:S(2)}) collective-permute-start(s16[272,512]{1,0:T(8,128)(2,1)S(1)} %get-tuple-element.30), channel_id=1, source_target_pairs={{0,40},{1,41},{2,42},{3,43},{4,44},{5,45},{6,46},{7,47},{8,48},{9,... | collective-permute-start | bytes 835592 | tf_op jit(solution)/shard_map/far_along_ring/ppermute | solution.py:258
  66.0 0.0 collective-permute-done.4.refs_0_
  66.0 14.1 %collective-permute-done.8.refs_1_ = s16[272,512]{1,0:T(8,128)(2,1)S(1)} collective-permute-done((s16[272,512]{1,0:T(8,128)(2,1)S(1)}, s16[272,512]{1,0:T(8,128)(2,1)S(1)}, u32[]{:S(2)}, u32[]{:S(2)}) %collective-permute-start.8) | collective-permute-done | bytes 278560 | tf_op jit(solution)/shard_map/far_along_ring/ppermute | solution.py:258
  80.1 6.5 %collective-permute-done.9.refs_2_ = s16[272,512]{1,0:T(8,128)(2,1)S(1)} collective-permute-done((s16[272,512]{1,0:T(8,128)(2,1)S(1)}, s16[272,512]{1,0:T(8,128)(2,1)S(1)}, u32[]{:S(2)}, u32[]{:S(2)}) %collective-permute-start.9) | collective-permute-done | bytes 278560 | tf_op jit(solution)/shard_map/far_along_ring/ppermute | solution.py:258
  86.6 0.9 along_line.2
  87.5 4.4 %collective-permute-start.10 = (s16[144,512]{1,0:T(8,128)(2,1)S(1)}, s16[144,512]{1,0:T(8,128)(2,1)S(1)}, u32[]{:S(2)}, u32[]{:S(2)}) collective-permute-start(s16[144,512]{1,0:T(8,128)(2,1)S(1)} %get-tuple-element.32), channel_id=1, source_target_pairs={{0,2},{1,3},{2,0},{3,1},{4,6},{5,7},{6,4},{7,5},{8,10},{9,11},{10,... | collective-permute-start | bytes 442376 | tf_op jit(solution)/shard_map/along_line/ppermute | solution.py:261
  91.9 7.1 %collective-permute-done.10.refs_0_ = s16[144,512]{1,0:T(8,128)(2,1)S(1)} collective-permute-done((s16[144,512]{1,0:T(8,128)(2,1)S(1)}, s16[144,512]{1,0:T(8,128)(2,1)S(1)}, u32[]{:S(2)}, u32[]{:S(2)}) %collective-permute-start.10) | collective-permute-done | bytes 147488 | tf_op jit(solution)/shard_map/along_line/ppermute | solution.py:261
  99.0 0.6 along_line.3
  99.7 6.4 %collective-permute-start.11 = (s16[80,512]{1,0:T(8,128)(2,1)S(1)}, s16[80,512]{1,0:T(8,128)(2,1)S(1)}, u32[]{:S(2)}, u32[]{:S(2)}) collective-permute-start(s16[80,512]{1,0:T(8,128)(2,1)S(1)} %get-tuple-element.34), channel_id=1, source_target_pairs={{0,4},{1,5},{2,6},{3,7},{4,0},{5,1},{6,2},{7,3},{8,12},{9,13},{10,... | collective-permute-start | bytes 245768 | tf_op jit(solution)/shard_map/along_line/ppermute | solution.py:261
  106.1 0.0 copy-done.2
  106.1 0.0 copy-done.3
  106.1 0.7 fusion.1
  106.8 6.4 %collective-permute-done.11.message = s16[80,512]{1,0:T(8,128)(2,1)S(1)} collective-permute-done((s16[80,512]{1,0:T(8,128)(2,1)S(1)}, s16[80,512]{1,0:T(8,128)(2,1)S(1)}, u32[]{:S(2)}, u32[]{:S(2)}) %collective-permute-start.11) | collective-permute-done | bytes 81952 | tf_op jit(solution)/shard_map/along_line/ppermute | solution.py:261
  113.3 1.2 %shard_map.87 = f32[64,512]{1,0:T(8,128)} custom-call(s32[4]{0:T(128)S(1)} %pad_add_fusion.place, f32[64,512]{1,0:T(8,128)S(1)} %get-tuple-element.33.kept, s16[80,512]{1,0:T(8,128)(2,1)S(1)} %collective-permute-done.11.message), custom_call_target="tpu_custom_call" | custom-call | bytes 3000000 | tf_op jit(solution)/shard_map/pallas_call | solution.py:162
  (8 shorter events, 0.1 us)
Async XLA Ops:
  0.6 38.3 %copy-start.1 = (bf16[1,256,512]{2,1,0:T(8,128)(2,1)S(1)}, bf16[1,256,512]{2,1,0:T(8,128)(2,1)}, u32[]{:S(2)}) copy-start(bf16[1,256,512]{2,1,0:T(8,128)(2,1)} %param.7) | copy-start | bytes 786436
  0.6 38.3 %copy-start = (bf16[1,256,4096]{2,1,0:T(8,128)(2,1)S(1)}, bf16[1,256,4096]{2,1,0:T(8,128)(2,1)}, u32[]{:S(2)}) copy-start(bf16[1,256,4096]{2,1,0:T(8,128)(2,1)} %param.6) | copy-start | bytes 6291460
  0.7 8.8 %copy-start.4 = (s32[8]{0:T(128)S(1)}, s32[8]{0:T(128)}, u32[]{:S(2)}) copy-start(s32[8]{0:T(128)} %param.11) | copy-start | bytes 100
  3.6 35.3 %collective-permute-start.3 = (bf16[256,1920]{1,0:T(8,128)(2,1)}, bf16[256,1920]{1,0:T(8,128)(2,1)S(1)}, u32[]{:S(2)}, u32[]{:S(2)}) collective-permute-start(bf16[256,1920]{1,0:T(8,128)(2,1)} %get-tuple-element.22), channel_id=1, source_target_pairs={{0,56},{1,57},{2,58},{3,59},{4,60},{5,61},{6,62},{7,63},{8,0},{9,1... | collective-permute-start | bytes 2949128 | tf_op jit(solution)/shard_map/inputs_to_neighbours/ppermute | solution.py:258
  5.9 33.0 %collective-permute-start.2 = (bf16[256,1664]{1,0:T(8,128)(2,1)}, bf16[256,1664]{1,0:T(8,128)(2,1)}, u32[]{:S(2)}, u32[]{:S(2)}) collective-permute-start(bf16[256,1664]{1,0:T(8,128)(2,1)} %get-tuple-element.19), channel_id=1, source_target_pairs={{0,8},{1,9},{2,10},{3,11},{4,12},{5,13},{6,14},{7,15},{8,16},{9,17... | collective-permute-start | bytes 2555912 | tf_op jit(solution)/shard_map/inputs_to_neighbours/ppermute | solution.py:258
  10.6 7.1 %collective-permute-start = (f32[2,2048]{1,0:T(2,128)S(1)}, f32[2,2048]{1,0:T(2,128)S(1)}, u32[]{:S(2)}, u32[]{:S(2)}) collective-permute-start(f32[2,2048]{1,0:T(2,128)S(1)} %pad_maximum_fusion), channel_id=1, source_target_pairs={{0,512},{64,576},{128,640},{192,704},{256,768},{320,832},{384,896}... | collective-permute-start | bytes 49160 | tf_op jit(solution)/shard_map/differences_over_replicas/ppermute | solution.py:237
  17.8 21.1 %collective-permute-start.1 = (f32[2,2048]{1,0:T(2,128)S(1)}, f32[2,2048]{1,0:T(2,128)S(1)}, u32[]{:S(2)}, u32[]{:S(2)}) collective-permute-start(f32[2,2048]{1,0:T(2,128)S(1)} %add.18), channel_id=1, source_target_pairs={{0,128},{64,192},{128,0},{192,64},{256,384},{320,448},{384,256},{4... | collective-permute-start | bytes 49160 | tf_op jit(solution)/shard_map/differences_over_replicas/ppermute | solution.py:237
  42.4 63.6 %copy-start.2 = (f32[8,2048]{1,0:T(8,128)S(1)}, f32[8,2048]{1,0:T(8,128)}, u32[]{:S(2)}) copy-start(f32[8,2048]{1,0:T(8,128)} %param.9) | copy-start | bytes 196612
  42.4 63.6 %copy-start.3 = (f32[8,2048]{1,0:T(8,128)S(1)}, f32[8,2048]{1,0:T(8,128)}, u32[]{:S(2)}) copy-start(f32[8,2048]{1,0:T(8,128)} %param.10) | copy-start | bytes 196612
  42.5 13.6 %collective-permute-start.7 = (s16[528,512]{1,0:T(8,128)(2,1)S(1)}, s16[528,512]{1,0:T(8,128)(2,1)S(1)}, u32[]{:S(2)}, u32[]{:S(2)}) collective-permute-start(s16[528,512]{1,0:T(8,128)(2,1)S(1)} %get-tuple-element.25), channel_id=1, source_target_pairs={{0,1},{1,0},{2,3},{3,2},{4,5},{5,4},{6,7},{7,6},{8,9},{9,8},{10,11... | collective-permute-start | bytes 1622024 | tf_op jit(solution)/shard_map/along_line_first/ppermute | solution.py:261
  46.0 3.1 %collective-permute-start.5 = (f32[2,2048]{1,0:T(2,128)S(1)}, f32[2,2048]{1,0:T(2,128)S(1)}, u32[]{:S(2)}, u32[]{:S(2)}) collective-permute-start(f32[2,2048]{1,0:T(2,128)S(1)} %add.19), channel_id=1, source_target_pairs={{0,64},{64,0},{128,192},{192,128},{256,320},{320,256},{384,448},{4... | collective-permute-start | bytes 49160 | tf_op jit(solution)/shard_map/differences_over_replicas/ppermute | solution.py:237
  49.1 5.9 %collective-permute-start.6 = (f32[2,2048]{1,0:T(2,128)S(1)}, f32[2,2048]{1,0:T(2,128)S(1)}, u32[]{:S(2)}, u32[]{:S(2)}) collective-permute-start(f32[2,2048]{1,0:T(2,128)S(1)} %add.20), channel_id=1, source_target_pairs={{0,256},{64,320},{128,384},{192,448},{256,0},{320,64},{384,128},{4... | collective-permute-start | bytes 49160 | tf_op jit(solution)/shard_map/differences_over_replicas/ppermute | solution.py:237
  52.5 13.5 %collective-permute-start.4 = (s16[272,512]{1,0:T(8,128)(2,1)S(1)}, s16[272,512]{1,0:T(8,128)(2,1)S(1)}, u32[]{:S(2)}, u32[]{:S(2)}) collective-permute-start(s16[272,512]{1,0:T(8,128)(2,1)S(1)} %get-tuple-element.24), channel_id=1, source_target_pairs={{0,1},{1,0},{2,3},{3,2},{4,5},{5,4},{6,7},{7,6},{8,9},{9,8},{10,11... | collective-permute-start | bytes 835592 | tf_op jit(solution)/shard_map/along_line_first/ppermute | solution.py:261
  57.1 23.0 %collective-permute-start.8 = (s16[272,512]{1,0:T(8,128)(2,1)S(1)}, s16[272,512]{1,0:T(8,128)(2,1)S(1)}, u32[]{:S(2)}, u32[]{:S(2)}) collective-permute-start(s16[272,512]{1,0:T(8,128)(2,1)S(1)} %get-tuple-element.29), channel_id=1, source_target_pairs={{0,24},{1,25},{2,26},{3,27},{4,28},{5,29},{6,30},{7,31},{8,32},{9,... | collective-permute-start | bytes 835592 | tf_op jit(solution)/shard_map/far_along_ring/ppermute | solution.py:258
  62.9 23.6 %collective-permute-start.9 = (s16[272,512]{1,0:T(8,128)(2,1)S(1)}, s16[272,512]{1,0:T(8,128)(2,1)S(1)}, u32[]{:S(2)}, u32[]{:S(2)}) collective-permute-start(s16[272,512]{1,0:T(8,128)(2,1)S(1)} %get-tuple-element.30), channel_id=1, source_target_pairs={{0,40},{1,41},{2,42},{3,43},{4,44},{5,45},{6,46},{7,47},{8,48},{9,... | collective-permute-start | bytes 835592 | tf_op jit(solution)/shard_map/far_along_ring/ppermute | solution.py:258
  87.5 11.6 %collective-permute-start.10 = (s16[144,512]{1,0:T(8,128)(2,1)S(1)}, s16[144,512]{1,0:T(8,128)(2,1)S(1)}, u32[]{:S(2)}, u32[]{:S(2)}) collective-permute-start(s16[144,512]{1,0:T(8,128)(2,1)S(1)} %get-tuple-element.32), channel_id=1, source_target_pairs={{0,2},{1,3},{2,0},{3,1},{4,6},{5,7},{6,4},{7,5},{8,10},{9,11},{10,... | collective-permute-start | bytes 442376 | tf_op jit(solution)/shard_map/along_line/ppermute | solution.py:261
  99.7 13.6 %collective-permute-start.11 = (s16[80,512]{1,0:T(8,128)(2,1)S(1)}, s16[80,512]{1,0:T(8,128)(2,1)S(1)}, u32[]{:S(2)}, u32[]{:S(2)}) collective-permute-start(s16[80,512]{1,0:T(8,128)(2,1)S(1)} %get-tuple-element.34), channel_id=1, source_target_pairs={{0,4},{1,5},{2,6},{3,7},{4,0},{5,1},{6,2},{7,3},{8,12},{9,13},{10,... | collective-permute-start | bytes 245768 | tf_op jit(solution)/shard_map/along_line/ppermute | solution.py:261

commit v5 on v4

--- a/solution.py
+++ b/solution.py
@@ -264,7 +264,7 @@
         above, below = pack(inputs, cotangent)
         received = [ring_move(above, 1), ring_move(below, -1)]
     picks, total, add_over = outer_sums(local, anchor, layer_fragment)
-    total = add_over(add_over(after(total, above), 8), 2)
+    total = add_over(after(total, above), 2)
     sent, kept, near, here = sums(after(place, total), inputs, cotangent, *received)
     with jax.named_scope("along_line_first"):
         arrived = line_move(sent, 1)
@@ -273,6 +273,7 @@
     up, down = rest(after(place, total), kept, arrived)
     with jax.named_scope("far_along_ring"):
         messages += [ring_move(up, 3), ring_move(down, -3)]
+    total = add_over(after(total, messages[1]), 8)
     with jax.named_scope("along_line"):
         sent, here = fold(place, 2, here, messages)
         sent = line_move(sent, 2)

time: 115 us -> 114 us (level)
  the two profiles are of different devices: /device:TPU:16 before, /device:TPU:51 now
where the time goes in v5:
time: 114 us; the launch traced here: 113 us
  starting transfers between devices  66.4 us (58%)
  waiting for transfers between devices  33.8 us (30%)
  Pallas kernels  10.2 us (9%)
  other arithmetic  2.06 us (2%)
    ppermute x4, starting transfers between devices, add_over(): lax.ppermute(total, 'rep', [(r, r ^ bit) for r in range(groups)])  31.1 us
    ppermute x4, starting transfers between devices, line_move(): return lax.ppermute(a, 'fsdp', along_line(bit))  22.5 us
    ppermute x4, waiting for transfers between devices, ring_move(): return lax.ppermute(a, 'fsdp', along_ring(shift))  15 us
    ppermute x4, waiting for transfers between devices, line_move(): return lax.ppermute(a, 'fsdp', along_line(bit))  14.4 us
    ppermute x4, starting transfers between devices, ring_move(): return lax.ppermute(a, 'fsdp', along_ring(shift))  12.7 us
    ppermute x4, waiting for transfers between devices, add_over(): lax.ppermute(total, 'rep', [(r, r ^ bit) for r in range(groups)])  4.45 us
    pallas_call x4, Pallas kernels, call(): pl.pallas_call(kernel, out_shape=[jax.ShapeDtypeStruct(s, d) for s, d in...  3.78 us
    pallas_call x1, Pallas kernels, on_chunks(): pl.pallas_call(kernel, out_shape=outs, grid_spec=pltpu.PrefetchScalarGrid...  3.49 us
  transfers between devices with their start and end apart: 12, of which 8 were waited for; matrix products, arithmetic and copies ran while one was open for 2% of the time, Pallas kernels for 1%

profile of v5, /device:TPU:51, one launch (start us, length us, event | category | flops | bytes accessed | tf_op | source)
XLA Modules:
  0.0 113.4 jit_solution(590094653064071133)
XLA Ops:
  0.6 0.0 copy-start.1
  0.6 0.0 copy-start
  0.7 0.0 copy-start.4
  0.7 2.9 %inputs_to_neighbours.1 = (bf16[256,1664]{1,0:T(8,128)(2,1)}, bf16[256,1920]{1,0:T(8,128)(2,1)}) custom-call(bf16[256,4096]{1,0:T(8,128)(2,1)} %bitcast.25, bf16[256,512]{1,0:T(8,128)(2,1)} %bitcast.29), custom_call_target="tpu_custom_call" | custom-call | tf_op jit(solution)/shard_map/inputs_to_neighbours/pallas_call | solution.py:113
  3.6 3.0 %collective-permute-start.2 = (bf16[256,1920]{1,0:T(8,128)(2,1)}, bf16[256,1920]{1,0:T(8,128)(2,1)S(1)}, u32[]{:S(2)}, u32[]{:S(2)}) collective-permute-start(bf16[256,1920]{1,0:T(8,128)(2,1)} %get-tuple-element.23), channel_id=1, source_target_pairs={{0,56},{1,57},{2,58},{3,59},{4,60},{5,61},{6,62},{7,63},{8,0},{9,1... | collective-permute-start | bytes 2949128 | tf_op jit(solution)/shard_map/inputs_to_neighbours/ppermute | solution.py:258
  6.5 2.3 %collective-permute-start.1 = (bf16[256,1664]{1,0:T(8,128)(2,1)}, bf16[256,1664]{1,0:T(8,128)(2,1)}, u32[]{:S(2)}, u32[]{:S(2)}) collective-permute-start(bf16[256,1664]{1,0:T(8,128)(2,1)} %get-tuple-element.20), channel_id=1, source_target_pairs={{0,8},{1,9},{2,10},{3,11},{4,12},{5,13},{6,14},{7,15},{8,16},{9,17... | collective-permute-start | bytes 2555912 | tf_op jit(solution)/shard_map/inputs_to_neighbours/ppermute | solution.py:258
  8.9 0.0 copy-done.4
  8.9 0.2 reduce-window.9
  9.1 1.0 select_reduce_fusion.1
  10.1 19.1 %collective-permute-start = (f32[2,2048]{1,0:T(2,128)S(1)}, f32[2,2048]{1,0:T(2,128)S(1)}, u32[]{:S(2)}, u32[]{:S(2)}) collective-permute-start(f32[2,2048]{1,0:T(2,128)S(1)} %pad_maximum_fusion), channel_id=1, source_target_pairs={{0,128},{64,192},{128,0},{192,64},{256,384},{320,448},{384,256},{4... | collective-permute-start | bytes 49160 | tf_op jit(solution)/shard_map/differences_over_replicas/ppermute | solution.py:237
  29.2 0.1 pad_add_fusion.place
  29.3 1.0 collective-permute-done
  30.3 0.0 collective-permute-done.1.below
  30.3 0.0 collective-permute-done.2.above
  30.3 0.0 copy-done.1
  30.3 0.0 copy-done
  30.3 3.5 %shard_map.85 = (s16[528,512]{1,0:T(8,128)(2,1)S(1)}, f32[512,512]{1,0:T(8,128)S(1)}, s16[272,512]{1,0:T(8,128)(2,1)S(1)}, f32[256,512]{1,0:T(8,128)S(1)}) custom-call(s32[4]{0:T(128)S(1)} %pad_add_fusion.place, bf16[256,4096]{1,0:T(8,128)(2,1)S(1)} %bitcast.26, bf16[256,4096]{1,0:T(8,128)(2,1)S(1)} %bitcast.27, bf16[256,4096]{1,0:T(8,128)(2,1)S(1)} %bitcast.28, ...), custom_call_target="tpu_custom_call" | custom-call | bytes 3000000 | tf_op jit(solution)/shard_map/pallas_call | solution.py:66
  33.9 0.0 copy-start.2
  33.9 0.0 copy-start.3
  33.9 3.2 %collective-permute-start.6 = (s16[528,512]{1,0:T(8,128)(2,1)S(1)}, s16[528,512]{1,0:T(8,128)(2,1)S(1)}, u32[]{:S(2)}, u32[]{:S(2)}) collective-permute-start(s16[528,512]{1,0:T(8,128)(2,1)S(1)} %get-tuple-element.26), channel_id=1, source_target_pairs={{0,1},{1,0},{2,3},{3,2},{4,5},{5,4},{6,7},{7,6},{8,9},{9,8},{10,11... | collective-permute-start | bytes 1622024 | tf_op jit(solution)/shard_map/along_line_first/ppermute | solution.py:261
  37.1 4.3 %collective-permute-start.4 = (f32[2,2048]{1,0:T(2,128)S(1)}, f32[2,2048]{1,0:T(2,128)S(1)}, u32[]{:S(2)}, u32[]{:S(2)}) collective-permute-start(f32[2,2048]{1,0:T(2,128)S(1)} %add.18), channel_id=1, source_target_pairs={{0,64},{64,0},{128,192},{192,128},{256,320},{320,256},{384,448},{4... | collective-permute-start | bytes 49160 | tf_op jit(solution)/shard_map/differences_over_replicas/ppermute | solution.py:237
  41.4 0.8 collective-permute-done.4
  42.2 2.2 %collective-permute-start.5 = (f32[2,2048]{1,0:T(2,128)S(1)}, f32[2,2048]{1,0:T(2,128)S(1)}, u32[]{:S(2)}, u32[]{:S(2)}) collective-permute-start(f32[2,2048]{1,0:T(2,128)S(1)} %add.19), channel_id=1, source_target_pairs={{0,256},{64,320},{128,384},{192,448},{256,0},{320,64},{384,128},{4... | collective-permute-start | bytes 49160 | tf_op jit(solution)/shard_map/differences_over_replicas/ppermute | solution.py:237
  44.4 2.6 %collective-permute-done.5 = f32[2,2048]{1,0:T(2,128)S(1)} collective-permute-done((f32[2,2048]{1,0:T(2,128)S(1)}, f32[2,2048]{1,0:T(2,128)S(1)}, u32[]{:S(2)}, u32[]{:S(2)}) %collective-permute-start.5) | collective-permute-done | bytes 16416 | tf_op jit(solution)/shard_map/differences_over_replicas/ppermute | solution.py:237
  47.0 0.9 collective-permute-done.6.message
  47.9 1.0 shard_map.86
  48.9 3.3 %collective-permute-start.7 = (s16[272,512]{1,0:T(8,128)(2,1)S(1)}, s16[272,512]{1,0:T(8,128)(2,1)S(1)}, u32[]{:S(2)}, u32[]{:S(2)}) collective-permute-start(s16[272,512]{1,0:T(8,128)(2,1)S(1)} %get-tuple-element.30), channel_id=1, source_target_pairs={{0,24},{1,25},{2,26},{3,27},{4,28},{5,29},{6,30},{7,31},{8,32},{9,... | collective-permute-start | bytes 835592 | tf_op jit(solution)/shard_map/far_along_ring/ppermute | solution.py:258
  52.3 3.6 %collective-permute-start.3 = (s16[272,512]{1,0:T(8,128)(2,1)S(1)}, s16[272,512]{1,0:T(8,128)(2,1)S(1)}, u32[]{:S(2)}, u32[]{:S(2)}) collective-permute-start(s16[272,512]{1,0:T(8,128)(2,1)S(1)} %get-tuple-element.25), channel_id=1, source_target_pairs={{0,1},{1,0},{2,3},{3,2},{4,5},{5,4},{6,7},{7,6},{8,9},{9,8},{10,11... | collective-permute-start | bytes 835592 | tf_op jit(solution)/shard_map/along_line_first/ppermute | solution.py:261
  55.9 4.0 %collective-permute-start.8 = (s16[272,512]{1,0:T(8,128)(2,1)S(1)}, s16[272,512]{1,0:T(8,128)(2,1)S(1)}, u32[]{:S(2)}, u32[]{:S(2)}) collective-permute-start(s16[272,512]{1,0:T(8,128)(2,1)S(1)} %get-tuple-element.31), channel_id=1, source_target_pairs={{0,40},{1,41},{2,42},{3,43},{4,44},{5,45},{6,46},{7,47},{8,48},{9,... | collective-permute-start | bytes 835592 | tf_op jit(solution)/shard_map/far_along_ring/ppermute | solution.py:258
  60.0 10.7 %collective-permute-done.7.refs_1_ = s16[272,512]{1,0:T(8,128)(2,1)S(1)} collective-permute-done((s16[272,512]{1,0:T(8,128)(2,1)S(1)}, s16[272,512]{1,0:T(8,128)(2,1)S(1)}, u32[]{:S(2)}, u32[]{:S(2)}) %collective-permute-start.7) | collective-permute-done | bytes 278560 | tf_op jit(solution)/shard_map/far_along_ring/ppermute | solution.py:258
  70.7 5.6 %collective-permute-start.11 = (f32[2,2048]{1,0:T(2,128)S(1)}, f32[2,2048]{1,0:T(2,128)S(1)}, u32[]{:S(2)}, u32[]{:S(2)}) collective-permute-start(f32[2,2048]{1,0:T(2,128)S(1)} %add.20), channel_id=1, source_target_pairs={{0,512},{64,576},{128,640},{192,704},{256,768},{320,832},{384,896}... | collective-permute-start | bytes 49160 | tf_op jit(solution)/shard_map/differences_over_replicas/ppermute | solution.py:237
  76.4 0.0 collective-permute-done.3.refs_0_
  76.4 4.3 %collective-permute-done.8.refs_2_ = s16[272,512]{1,0:T(8,128)(2,1)S(1)} collective-permute-done((s16[272,512]{1,0:T(8,128)(2,1)S(1)}, s16[272,512]{1,0:T(8,128)(2,1)S(1)}, u32[]{:S(2)}, u32[]{:S(2)}) %collective-permute-start.8) | collective-permute-done | bytes 278560 | tf_op jit(solution)/shard_map/far_along_ring/ppermute | solution.py:258
  80.6 0.9 along_line.2
  81.5 5.2 %collective-permute-start.9 = (s16[144,512]{1,0:T(8,128)(2,1)S(1)}, s16[144,512]{1,0:T(8,128)(2,1)S(1)}, u32[]{:S(2)}, u32[]{:S(2)}) collective-permute-start(s16[144,512]{1,0:T(8,128)(2,1)S(1)} %get-tuple-element.33), channel_id=1, source_target_pairs={{0,2},{1,3},{2,0},{3,1},{4,6},{5,7},{6,4},{7,5},{8,10},{9,11},{10,... | collective-permute-start | bytes 442376 | tf_op jit(solution)/shard_map/along_line/ppermute | solution.py:261
  86.7 0.0 collective-permute-done.11
  86.7 7.4 %collective-permute-done.9.refs_0_ = s16[144,512]{1,0:T(8,128)(2,1)S(1)} collective-permute-done((s16[144,512]{1,0:T(8,128)(2,1)S(1)}, s16[144,512]{1,0:T(8,128)(2,1)S(1)}, u32[]{:S(2)}, u32[]{:S(2)}) %collective-permute-start.9) | collective-permute-done | bytes 147488 | tf_op jit(solution)/shard_map/along_line/ppermute | solution.py:261
  94.1 0.6 along_line.3
  94.8 10.5 %collective-permute-start.10 = (s16[80,512]{1,0:T(8,128)(2,1)S(1)}, s16[80,512]{1,0:T(8,128)(2,1)S(1)}, u32[]{:S(2)}, u32[]{:S(2)}) collective-permute-start(s16[80,512]{1,0:T(8,128)(2,1)S(1)} %get-tuple-element.35), channel_id=1, source_target_pairs={{0,4},{1,5},{2,6},{3,7},{4,0},{5,1},{6,2},{7,3},{8,12},{9,13},{10,... | collective-permute-start | bytes 245768 | tf_op jit(solution)/shard_map/along_line/ppermute | solution.py:261
  105.3 0.0 copy-done.2
  105.3 0.0 copy-done.3
  105.3 0.7 fusion.1
  106.1 6.1 %collective-permute-done.10.message = s16[80,512]{1,0:T(8,128)(2,1)S(1)} collective-permute-done((s16[80,512]{1,0:T(8,128)(2,1)S(1)}, s16[80,512]{1,0:T(8,128)(2,1)S(1)}, u32[]{:S(2)}, u32[]{:S(2)}) %collective-permute-start.10) | collective-permute-done | bytes 81952 | tf_op jit(solution)/shard_map/along_line/ppermute | solution.py:261
  112.2 1.2 %shard_map.87 = f32[64,512]{1,0:T(8,128)} custom-call(s32[4]{0:T(128)S(1)} %pad_add_fusion.place, f32[64,512]{1,0:T(8,128)S(1)} %get-tuple-element.34.kept, s16[80,512]{1,0:T(8,128)(2,1)S(1)} %collective-permute-done.10.message), custom_call_target="tpu_custom_call" | custom-call | bytes 3000000 | tf_op jit(solution)/shard_map/pallas_call | solution.py:162
  (8 shorter events, 0.1 us)
Async XLA Ops:
  0.6 29.7 %copy-start.1 = (bf16[1,256,512]{2,1,0:T(8,128)(2,1)S(1)}, bf16[1,256,512]{2,1,0:T(8,128)(2,1)}, u32[]{:S(2)}) copy-start(bf16[1,256,512]{2,1,0:T(8,128)(2,1)} %param.7) | copy-start | bytes 786436
  0.6 29.7 %copy-start = (bf16[1,256,4096]{2,1,0:T(8,128)(2,1)S(1)}, bf16[1,256,4096]{2,1,0:T(8,128)(2,1)}, u32[]{:S(2)}) copy-start(bf16[1,256,4096]{2,1,0:T(8,128)(2,1)} %param.6) | copy-start | bytes 6291460
  0.7 8.2 %copy-start.4 = (s32[8]{0:T(128)S(1)}, s32[8]{0:T(128)}, u32[]{:S(2)}) copy-start(s32[8]{0:T(128)} %param.11) | copy-start | bytes 100
  3.6 26.8 %collective-permute-start.2 = (bf16[256,1920]{1,0:T(8,128)(2,1)}, bf16[256,1920]{1,0:T(8,128)(2,1)S(1)}, u32[]{:S(2)}, u32[]{:S(2)}) collective-permute-start(bf16[256,1920]{1,0:T(8,128)(2,1)} %get-tuple-element.23), channel_id=1, source_target_pairs={{0,56},{1,57},{2,58},{3,59},{4,60},{5,61},{6,62},{7,63},{8,0},{9,1... | collective-permute-start | bytes 2949128 | tf_op jit(solution)/shard_map/inputs_to_neighbours/ppermute | solution.py:258
  6.5 23.8 %collective-permute-start.1 = (bf16[256,1664]{1,0:T(8,128)(2,1)}, bf16[256,1664]{1,0:T(8,128)(2,1)}, u32[]{:S(2)}, u32[]{:S(2)}) collective-permute-start(bf16[256,1664]{1,0:T(8,128)(2,1)} %get-tuple-element.20), channel_id=1, source_target_pairs={{0,8},{1,9},{2,10},{3,11},{4,12},{5,13},{6,14},{7,15},{8,16},{9,17... | collective-permute-start | bytes 2555912 | tf_op jit(solution)/shard_map/inputs_to_neighbours/ppermute | solution.py:258
  10.1 20.2 %collective-permute-start = (f32[2,2048]{1,0:T(2,128)S(1)}, f32[2,2048]{1,0:T(2,128)S(1)}, u32[]{:S(2)}, u32[]{:S(2)}) collective-permute-start(f32[2,2048]{1,0:T(2,128)S(1)} %pad_maximum_fusion), channel_id=1, source_target_pairs={{0,128},{64,192},{128,0},{192,64},{256,384},{320,448},{384,256},{4... | collective-permute-start | bytes 49160 | tf_op jit(solution)/shard_map/differences_over_replicas/ppermute | solution.py:237
  33.9 71.5 %copy-start.2 = (f32[8,2048]{1,0:T(8,128)S(1)}, f32[8,2048]{1,0:T(8,128)}, u32[]{:S(2)}) copy-start(f32[8,2048]{1,0:T(8,128)} %param.9) | copy-start | bytes 196612
  33.9 71.5 %copy-start.3 = (f32[8,2048]{1,0:T(8,128)S(1)}, f32[8,2048]{1,0:T(8,128)}, u32[]{:S(2)}) copy-start(f32[8,2048]{1,0:T(8,128)} %param.10) | copy-start | bytes 196612
  33.9 14.0 %collective-permute-start.6 = (s16[528,512]{1,0:T(8,128)(2,1)S(1)}, s16[528,512]{1,0:T(8,128)(2,1)S(1)}, u32[]{:S(2)}, u32[]{:S(2)}) collective-permute-start(s16[528,512]{1,0:T(8,128)(2,1)S(1)} %get-tuple-element.26), channel_id=1, source_target_pairs={{0,1},{1,0},{2,3},{3,2},{4,5},{5,4},{6,7},{7,6},{8,9},{9,8},{10,11... | collective-permute-start | bytes 1622024 | tf_op jit(solution)/shard_map/along_line_first/ppermute | solution.py:261
  37.1 5.1 %collective-permute-start.4 = (f32[2,2048]{1,0:T(2,128)S(1)}, f32[2,2048]{1,0:T(2,128)S(1)}, u32[]{:S(2)}, u32[]{:S(2)}) collective-permute-start(f32[2,2048]{1,0:T(2,128)S(1)} %add.18), channel_id=1, source_target_pairs={{0,64},{64,0},{128,192},{192,128},{256,320},{320,256},{384,448},{4... | collective-permute-start | bytes 49160 | tf_op jit(solution)/shard_map/differences_over_replicas/ppermute | solution.py:237
  42.2 4.8 %collective-permute-start.5 = (f32[2,2048]{1,0:T(2,128)S(1)}, f32[2,2048]{1,0:T(2,128)S(1)}, u32[]{:S(2)}, u32[]{:S(2)}) collective-permute-start(f32[2,2048]{1,0:T(2,128)S(1)} %add.19), channel_id=1, source_target_pairs={{0,256},{64,320},{128,384},{192,448},{256,0},{320,64},{384,128},{4... | collective-permute-start | bytes 49160 | tf_op jit(solution)/shard_map/differences_over_replicas/ppermute | solution.py:237
  48.9 21.8 %collective-permute-start.7 = (s16[272,512]{1,0:T(8,128)(2,1)S(1)}, s16[272,512]{1,0:T(8,128)(2,1)S(1)}, u32[]{:S(2)}, u32[]{:S(2)}) collective-permute-start(s16[272,512]{1,0:T(8,128)(2,1)S(1)} %get-tuple-element.30), channel_id=1, source_target_pairs={{0,24},{1,25},{2,26},{3,27},{4,28},{5,29},{6,30},{7,31},{8,32},{9,... | collective-permute-start | bytes 835592 | tf_op jit(solution)/shard_map/far_along_ring/ppermute | solution.py:258
  52.3 24.1 %collective-permute-start.3 = (s16[272,512]{1,0:T(8,128)(2,1)S(1)}, s16[272,512]{1,0:T(8,128)(2,1)S(1)}, u32[]{:S(2)}, u32[]{:S(2)}) collective-permute-start(s16[272,512]{1,0:T(8,128)(2,1)S(1)} %get-tuple-element.25), channel_id=1, source_target_pairs={{0,1},{1,0},{2,3},{3,2},{4,5},{5,4},{6,7},{7,6},{8,9},{9,8},{10,11... | collective-permute-start | bytes 835592 | tf_op jit(solution)/shard_map/along_line_first/ppermute | solution.py:261
  55.9 24.7 %collective-permute-start.8 = (s16[272,512]{1,0:T(8,128)(2,1)S(1)}, s16[272,512]{1,0:T(8,128)(2,1)S(1)}, u32[]{:S(2)}, u32[]{:S(2)}) collective-permute-start(s16[272,512]{1,0:T(8,128)(2,1)S(1)} %get-tuple-element.31), channel_id=1, source_target_pairs={{0,40},{1,41},{2,42},{3,43},{4,44},{5,45},{6,46},{7,47},{8,48},{9,... | collective-permute-start | bytes 835592 | tf_op jit(solution)/shard_map/far_along_ring/ppermute | solution.py:258
  70.7 16.0 %collective-permute-start.11 = (f32[2,2048]{1,0:T(2,128)S(1)}, f32[2,2048]{1,0:T(2,128)S(1)}, u32[]{:S(2)}, u32[]{:S(2)}) collective-permute-start(f32[2,2048]{1,0:T(2,128)S(1)} %add.20), channel_id=1, source_target_pairs={{0,512},{64,576},{128,640},{192,704},{256,768},{320,832},{384,896}... | collective-permute-start | bytes 49160 | tf_op jit(solution)/shard_map/differences_over_replicas/ppermute | solution.py:237
  81.5 12.6 %collective-permute-start.9 = (s16[144,512]{1,0:T(8,128)(2,1)S(1)}, s16[144,512]{1,0:T(8,128)(2,1)S(1)}, u32[]{:S(2)}, u32[]{:S(2)}) collective-permute-start(s16[144,512]{1,0:T(8,128)(2,1)S(1)} %get-tuple-element.33), channel_id=1, source_target_pairs={{0,2},{1,3},{2,0},{3,1},{4,6},{5,7},{6,4},{7,5},{8,10},{9,11},{10,... | collective-permute-start | bytes 442376 | tf_op jit(solution)/shard_map/along_line/ppermute | solution.py:261
  94.8 17.4 %collective-permute-start.10 = (s16[80,512]{1,0:T(8,128)(2,1)S(1)}, s16[80,512]{1,0:T(8,128)(2,1)S(1)}, u32[]{:S(2)}, u32[]{:S(2)}) collective-permute-start(s16[80,512]{1,0:T(8,128)(2,1)S(1)} %get-tuple-element.35), channel_id=1, source_target_pairs={{0,4},{1,5},{2,6},{3,7},{4,0},{5,1},{6,2},{7,3},{8,12},{9,13},{10,... | collective-permute-start | bytes 245768 | tf_op jit(solution)/shard_map/along_line/ppermute | solution.py:261

commit v6 on v5

--- a/solution.py
+++ b/solution.py
@@ -268,12 +268,13 @@
     sent, kept, near, here = sums(after(place, total), inputs, cotangent, *received)
     with jax.named_scope("along_line_first"):
         arrived = line_move(sent, 1)
-        messages = [line_move(near, 1)]
     total = add_over(add_over(after(total, sent), 1), 4)
+    with jax.named_scope("near_along_line"):
+        messages = [line_move(after(near, total), 1)]
     up, down = rest(after(place, total), kept, arrived)
     with jax.named_scope("far_along_ring"):
         messages += [ring_move(up, 3), ring_move(down, -3)]
-    total = add_over(after(total, messages[1]), 8)
+    total = add_over(after(total, messages[0], messages[1]), 8)
     with jax.named_scope("along_line"):
         sent, here = fold(place, 2, here, messages)
         sent = line_move(sent, 2)

time: 114 us -> 113 us (level)
  the two profiles are of different devices: /device:TPU:51 before, /device:TPU:22 now
where the time goes in v6:
time: 113 us
  starting transfers between devices  63 us (56%)
  waiting for transfers between devices  36.7 us (32%)
  Pallas kernels  10.2 us (9%)
  other arithmetic  2.06 us (2%)
    ppermute x4, starting transfers between devices, add_over(): lax.ppermute(total, 'rep', [(r, r ^ bit) for r in range(groups)])  26.8 us
    ppermute x4, starting transfers between devices, line_move(): return lax.ppermute(a, 'fsdp', along_line(bit))  21.4 us
    ppermute x4, waiting for transfers between devices, ring_move(): return lax.ppermute(a, 'fsdp', along_ring(shift))  18.2 us
    ppermute x4, starting transfers between devices, ring_move(): return lax.ppermute(a, 'fsdp', along_ring(shift))  14.7 us
    ppermute x4, waiting for transfers between devices, line_move(): return lax.ppermute(a, 'fsdp', along_line(bit))  12.8 us
    ppermute x4, waiting for transfers between devices, add_over(): lax.ppermute(total, 'rep', [(r, r ^ bit) for r in range(groups)])  5.65 us
    pallas_call x4, Pallas kernels, call(): pl.pallas_call(kernel, out_shape=[jax.ShapeDtypeStruct(s, d) for s, d in...  3.78 us
    pallas_call x1, Pallas kernels, on_chunks(): pl.pallas_call(kernel, out_shape=outs, grid_spec=pltpu.PrefetchScalarGrid...  3.5 us
  transfers between devices with their start and end apart: 12, of which 8 were waited for; matrix products, arithmetic and copies ran while one was open for 2% of the time, Pallas kernels for 2%

profile of v6, /device:TPU:22, one launch (start us, length us, event | category | flops | bytes accessed | tf_op | source)
XLA Modules:
  0.0 112.8 jit_solution(12221018674598001726)
XLA Ops:
  0.6 0.0 copy-start.1
  0.6 0.0 copy-start
  0.7 0.0 copy-start.4
  0.7 2.9 %inputs_to_neighbours.1 = (bf16[256,1664]{1,0:T(8,128)(2,1)}, bf16[256,1920]{1,0:T(8,128)(2,1)}) custom-call(bf16[256,4096]{1,0:T(8,128)(2,1)} %bitcast.25, bf16[256,512]{1,0:T(8,128)(2,1)} %bitcast.29), custom_call_target="tpu_custom_call" | custom-call | tf_op jit(solution)/shard_map/inputs_to_neighbours/pallas_call | solution.py:113
  3.6 2.4 %collective-permute-start.2 = (bf16[256,1920]{1,0:T(8,128)(2,1)}, bf16[256,1920]{1,0:T(8,128)(2,1)S(1)}, u32[]{:S(2)}, u32[]{:S(2)}) collective-permute-start(bf16[256,1920]{1,0:T(8,128)(2,1)} %get-tuple-element.24), channel_id=1, source_target_pairs={{0,56},{1,57},{2,58},{3,59},{4,60},{5,61},{6,62},{7,63},{8,0},{9,1... | collective-permute-start | bytes 2949128 | tf_op jit(solution)/shard_map/inputs_to_neighbours/ppermute | solution.py:258
  5.9 3.5 %collective-permute-start.1 = (bf16[256,1664]{1,0:T(8,128)(2,1)}, bf16[256,1664]{1,0:T(8,128)(2,1)}, u32[]{:S(2)}, u32[]{:S(2)}) collective-permute-start(bf16[256,1664]{1,0:T(8,128)(2,1)} %get-tuple-element.21), channel_id=1, source_target_pairs={{0,8},{1,9},{2,10},{3,11},{4,12},{5,13},{6,14},{7,15},{8,16},{9,17... | collective-permute-start | bytes 2555912 | tf_op jit(solution)/shard_map/inputs_to_neighbours/ppermute | solution.py:258
  9.4 0.0 copy-done.4
  9.4 0.2 reduce-window.9
  9.6 1.0 select_reduce_fusion.1
  10.6 19.4 %collective-permute-start = (f32[2,2048]{1,0:T(2,128)S(1)}, f32[2,2048]{1,0:T(2,128)S(1)}, u32[]{:S(2)}, u32[]{:S(2)}) collective-permute-start(f32[2,2048]{1,0:T(2,128)S(1)} %pad_maximum_fusion), channel_id=1, source_target_pairs={{0,128},{64,192},{128,0},{192,64},{256,384},{320,448},{384,256},{4... | collective-permute-start | bytes 49160 | tf_op jit(solution)/shard_map/differences_over_replicas/ppermute | solution.py:237
  30.0 0.1 pad_add_fusion.place
  30.1 1.6 %collective-permute-done = f32[2,2048]{1,0:T(2,128)S(1)} collective-permute-done((f32[2,2048]{1,0:T(2,128)S(1)}, f32[2,2048]{1,0:T(2,128)S(1)}, u32[]{:S(2)}, u32[]{:S(2)}) %collective-permute-start) | collective-permute-done | bytes 16416 | tf_op jit(solution)/shard_map/differences_over_replicas/ppermute | solution.py:237
  31.7 0.0 collective-permute-done.1.below
  31.7 0.0 collective-permute-done.2.above
  31.8 0.0 copy-done.1
  31.8 0.0 copy-done
  31.8 3.5 %shard_map.85 = (s16[528,512]{1,0:T(8,128)(2,1)S(1)}, f32[512,512]{1,0:T(8,128)S(1)}, s16[272,512]{1,0:T(8,128)(2,1)S(1)}, f32[256,512]{1,0:T(8,128)S(1)}) custom-call(s32[4]{0:T(128)S(1)} %pad_add_fusion.place, bf16[256,4096]{1,0:T(8,128)(2,1)S(1)} %bitcast.26, bf16[256,4096]{1,0:T(8,128)(2,1)S(1)} %bitcast.27, bf16[256,4096]{1,0:T(8,128)(2,1)S(1)} %bitcast.28, ...), custom_call_target="tpu_custom_call" | custom-call | bytes 3000000 | tf_op jit(solution)/shard_map/pallas_call | solution.py:66
  35.3 0.0 copy-start.2
  35.3 0.0 copy-start.3
  35.3 3.5 %collective-permute-start.6 = (s16[528,512]{1,0:T(8,128)(2,1)S(1)}, s16[528,512]{1,0:T(8,128)(2,1)S(1)}, u32[]{:S(2)}, u32[]{:S(2)}) collective-permute-start(s16[528,512]{1,0:T(8,128)(2,1)S(1)} %get-tuple-element.27), channel_id=1, source_target_pairs={{0,1},{1,0},{2,3},{3,2},{4,5},{5,4},{6,7},{7,6},{8,9},{9,8},{10,11... | collective-permute-start | bytes 1622024 | tf_op jit(solution)/shard_map/along_line_first/ppermute | solution.py:261
  38.8 1.9 %collective-permute-start.3 = (f32[2,2048]{1,0:T(2,128)S(1)}, f32[2,2048]{1,0:T(2,128)S(1)}, u32[]{:S(2)}, u32[]{:S(2)}) collective-permute-start(f32[2,2048]{1,0:T(2,128)S(1)} %add.18), channel_id=1, source_target_pairs={{0,64},{64,0},{128,192},{192,128},{256,320},{320,256},{384,448},{4... | collective-permute-start | bytes 49160 | tf_op jit(solution)/shard_map/differences_over_replicas/ppermute | solution.py:237
  40.7 1.1 %collective-permute-done.3 = f32[2,2048]{1,0:T(2,128)S(1)} collective-permute-done((f32[2,2048]{1,0:T(2,128)S(1)}, f32[2,2048]{1,0:T(2,128)S(1)}, u32[]{:S(2)}, u32[]{:S(2)}) %collective-permute-start.3) | collective-permute-done | bytes 16416 | tf_op jit(solution)/shard_map/differences_over_replicas/ppermute | solution.py:237
  41.9 2.7 %collective-permute-start.4 = (f32[2,2048]{1,0:T(2,128)S(1)}, f32[2,2048]{1,0:T(2,128)S(1)}, u32[]{:S(2)}, u32[]{:S(2)}) collective-permute-start(f32[2,2048]{1,0:T(2,128)S(1)} %add.19), channel_id=1, source_target_pairs={{0,256},{64,320},{128,384},{192,448},{256,0},{320,64},{384,128},{4... | collective-permute-start | bytes 49160 | tf_op jit(solution)/shard_map/differences_over_replicas/ppermute | solution.py:237
  44.6 2.9 %collective-permute-done.4 = f32[2,2048]{1,0:T(2,128)S(1)} collective-permute-done((f32[2,2048]{1,0:T(2,128)S(1)}, f32[2,2048]{1,0:T(2,128)S(1)}, u32[]{:S(2)}, u32[]{:S(2)}) %collective-permute-start.4) | collective-permute-done | bytes 16416 | tf_op jit(solution)/shard_map/differences_over_replicas/ppermute | solution.py:237
  47.6 2.5 %collective-permute-start.5 = (s16[272,512]{1,0:T(8,128)(2,1)S(1)}, s16[272,512]{1,0:T(8,128)(2,1)S(1)}, u32[]{:S(2)}, u32[]{:S(2)}) collective-permute-start(s16[272,512]{1,0:T(8,128)(2,1)S(1)} %get-tuple-element.29), channel_id=1, source_target_pairs={{0,1},{1,0},{2,3},{3,2},{4,5},{5,4},{6,7},{7,6},{8,9},{9,8},{10,11... | collective-permute-start | bytes 835592 | tf_op jit(solution)/shard_map/near_along_line/ppermute | solution.py:261
  50.0 0.1 collective-permute-done.6.message
  50.1 1.0 shard_map.86
  51.1 5.8 %collective-permute-start.7 = (s16[272,512]{1,0:T(8,128)(2,1)S(1)}, s16[272,512]{1,0:T(8,128)(2,1)S(1)}, u32[]{:S(2)}, u32[]{:S(2)}) collective-permute-start(s16[272,512]{1,0:T(8,128)(2,1)S(1)} %get-tuple-element.32), channel_id=1, source_target_pairs={{0,24},{1,25},{2,26},{3,27},{4,28},{5,29},{6,30},{7,31},{8,32},{9,... | collective-permute-start | bytes 835592 | tf_op jit(solution)/shard_map/far_along_ring/ppermute | solution.py:258
  56.9 3.0 %collective-permute-start.8 = (s16[272,512]{1,0:T(8,128)(2,1)S(1)}, s16[272,512]{1,0:T(8,128)(2,1)S(1)}, u32[]{:S(2)}, u32[]{:S(2)}) collective-permute-start(s16[272,512]{1,0:T(8,128)(2,1)S(1)} %get-tuple-element.33), channel_id=1, source_target_pairs={{0,40},{1,41},{2,42},{3,43},{4,44},{5,45},{6,46},{7,47},{8,48},{9,... | collective-permute-start | bytes 835592 | tf_op jit(solution)/shard_map/far_along_ring/ppermute | solution.py:258
  60.0 0.0 collective-permute-done.5.refs_0_
  60.0 15.1 %collective-permute-done.7.refs_1_ = s16[272,512]{1,0:T(8,128)(2,1)S(1)} collective-permute-done((s16[272,512]{1,0:T(8,128)(2,1)S(1)}, s16[272,512]{1,0:T(8,128)(2,1)S(1)}, u32[]{:S(2)}, u32[]{:S(2)}) %collective-permute-start.7) | collective-permute-done | bytes 278560 | tf_op jit(solution)/shard_map/far_along_ring/ppermute | solution.py:258
  75.0 2.8 %collective-permute-start.11 = (f32[2,2048]{1,0:T(2,128)S(1)}, f32[2,2048]{1,0:T(2,128)S(1)}, u32[]{:S(2)}, u32[]{:S(2)}) collective-permute-start(f32[2,2048]{1,0:T(2,128)S(1)} %add.20), channel_id=1, source_target_pairs={{0,512},{64,576},{128,640},{192,704},{256,768},{320,832},{384,896}... | collective-permute-start | bytes 49160 | tf_op jit(solution)/shard_map/differences_over_replicas/ppermute | solution.py:237
  77.9 3.2 %collective-permute-done.8.refs_2_ = s16[272,512]{1,0:T(8,128)(2,1)S(1)} collective-permute-done((s16[272,512]{1,0:T(8,128)(2,1)S(1)}, s16[272,512]{1,0:T(8,128)(2,1)S(1)}, u32[]{:S(2)}, u32[]{:S(2)}) %collective-permute-start.8) | collective-permute-done | bytes 278560 | tf_op jit(solution)/shard_map/far_along_ring/ppermute | solution.py:258
  81.0 0.9 along_line.2
  81.9 4.5 %collective-permute-start.9 = (s16[144,512]{1,0:T(8,128)(2,1)S(1)}, s16[144,512]{1,0:T(8,128)(2,1)S(1)}, u32[]{:S(2)}, u32[]{:S(2)}) collective-permute-start(s16[144,512]{1,0:T(8,128)(2,1)S(1)} %get-tuple-element.35), channel_id=1, source_target_pairs={{0,2},{1,3},{2,0},{3,1},{4,6},{5,7},{6,4},{7,5},{8,10},{9,11},{10,... | collective-permute-start | bytes 442376 | tf_op jit(solution)/shard_map/along_line/ppermute | solution.py:261
  86.4 0.0 collective-permute-done.11
  86.5 7.0 %collective-permute-done.9.refs_0_ = s16[144,512]{1,0:T(8,128)(2,1)S(1)} collective-permute-done((s16[144,512]{1,0:T(8,128)(2,1)S(1)}, s16[144,512]{1,0:T(8,128)(2,1)S(1)}, u32[]{:S(2)}, u32[]{:S(2)}) %collective-permute-start.9) | collective-permute-done | bytes 147488 | tf_op jit(solution)/shard_map/along_line/ppermute | solution.py:261
  93.5 0.6 along_line.3
  94.2 11.0 %collective-permute-start.10 = (s16[80,512]{1,0:T(8,128)(2,1)S(1)}, s16[80,512]{1,0:T(8,128)(2,1)S(1)}, u32[]{:S(2)}, u32[]{:S(2)}) collective-permute-start(s16[80,512]{1,0:T(8,128)(2,1)S(1)} %get-tuple-element.37), channel_id=1, source_target_pairs={{0,4},{1,5},{2,6},{3,7},{4,0},{5,1},{6,2},{7,3},{8,12},{9,13},{10,... | collective-permute-start | bytes 245768 | tf_op jit(solution)/shard_map/along_line/ppermute | solution.py:261
  105.1 0.0 copy-done.2
  105.1 0.0 copy-done.3
  105.2 0.7 fusion.1
  105.9 5.7 %collective-permute-done.10.message = s16[80,512]{1,0:T(8,128)(2,1)S(1)} collective-permute-done((s16[80,512]{1,0:T(8,128)(2,1)S(1)}, s16[80,512]{1,0:T(8,128)(2,1)S(1)}, u32[]{:S(2)}, u32[]{:S(2)}) %collective-permute-start.10) | collective-permute-done | bytes 81952 | tf_op jit(solution)/shard_map/along_line/ppermute | solution.py:261
  111.6 1.2 %shard_map.87 = f32[64,512]{1,0:T(8,128)} custom-call(s32[4]{0:T(128)S(1)} %pad_add_fusion.place, f32[64,512]{1,0:T(8,128)S(1)} %get-tuple-element.36.kept, s16[80,512]{1,0:T(8,128)(2,1)S(1)} %collective-permute-done.10.message), custom_call_target="tpu_custom_call" | custom-call | bytes 3000000 | tf_op jit(solution)/shard_map/pallas_call | solution.py:162
  (8 shorter events, 0.1 us)
Async XLA Ops:
  0.6 31.1 %copy-start.1 = (bf16[1,256,512]{2,1,0:T(8,128)(2,1)S(1)}, bf16[1,256,512]{2,1,0:T(8,128)(2,1)}, u32[]{:S(2)}) copy-start(bf16[1,256,512]{2,1,0:T(8,128)(2,1)} %param.7) | copy-start | bytes 786436
  0.6 31.1 %copy-start = (bf16[1,256,4096]{2,1,0:T(8,128)(2,1)S(1)}, bf16[1,256,4096]{2,1,0:T(8,128)(2,1)}, u32[]{:S(2)}) copy-start(bf16[1,256,4096]{2,1,0:T(8,128)(2,1)} %param.6) | copy-start | bytes 6291460
  0.7 8.8 %copy-start.4 = (s32[8]{0:T(128)S(1)}, s32[8]{0:T(128)}, u32[]{:S(2)}) copy-start(s32[8]{0:T(128)} %param.11) | copy-start | bytes 100
  3.6 28.2 %collective-permute-start.2 = (bf16[256,1920]{1,0:T(8,128)(2,1)}, bf16[256,1920]{1,0:T(8,128)(2,1)S(1)}, u32[]{:S(2)}, u32[]{:S(2)}) collective-permute-start(bf16[256,1920]{1,0:T(8,128)(2,1)} %get-tuple-element.24), channel_id=1, source_target_pairs={{0,56},{1,57},{2,58},{3,59},{4,60},{5,61},{6,62},{7,63},{8,0},{9,1... | collective-permute-start | bytes 2949128 | tf_op jit(solution)/shard_map/inputs_to_neighbours/ppermute | solution.py:258
  5.9 25.8 %collective-permute-start.1 = (bf16[256,1664]{1,0:T(8,128)(2,1)}, bf16[256,1664]{1,0:T(8,128)(2,1)}, u32[]{:S(2)}, u32[]{:S(2)}) collective-permute-start(bf16[256,1664]{1,0:T(8,128)(2,1)} %get-tuple-element.21), channel_id=1, source_target_pairs={{0,8},{1,9},{2,10},{3,11},{4,12},{5,13},{6,14},{7,15},{8,16},{9,17... | collective-permute-start | bytes 2555912 | tf_op jit(solution)/shard_map/inputs_to_neighbours/ppermute | solution.py:258
  10.6 21.1 %collective-permute-start = (f32[2,2048]{1,0:T(2,128)S(1)}, f32[2,2048]{1,0:T(2,128)S(1)}, u32[]{:S(2)}, u32[]{:S(2)}) collective-permute-start(f32[2,2048]{1,0:T(2,128)S(1)} %pad_maximum_fusion), channel_id=1, source_target_pairs={{0,128},{64,192},{128,0},{192,64},{256,384},{320,448},{384,256},{4... | collective-permute-start | bytes 49160 | tf_op jit(solution)/shard_map/differences_over_replicas/ppermute | solution.py:237
  35.3 69.9 %copy-start.2 = (f32[8,2048]{1,0:T(8,128)S(1)}, f32[8,2048]{1,0:T(8,128)}, u32[]{:S(2)}) copy-start(f32[8,2048]{1,0:T(8,128)} %param.9) | copy-start | bytes 196612
  35.3 69.8 %copy-start.3 = (f32[8,2048]{1,0:T(8,128)S(1)}, f32[8,2048]{1,0:T(8,128)}, u32[]{:S(2)}) copy-start(f32[8,2048]{1,0:T(8,128)} %param.10) | copy-start | bytes 196612
  35.3 14.8 %collective-permute-start.6 = (s16[528,512]{1,0:T(8,128)(2,1)S(1)}, s16[528,512]{1,0:T(8,128)(2,1)S(1)}, u32[]{:S(2)}, u32[]{:S(2)}) collective-permute-start(s16[528,512]{1,0:T(8,128)(2,1)S(1)} %get-tuple-element.27), channel_id=1, source_target_pairs={{0,1},{1,0},{2,3},{3,2},{4,5},{5,4},{6,7},{7,6},{8,9},{9,8},{10,11... | collective-permute-start | bytes 1622024 | tf_op jit(solution)/shard_map/along_line_first/ppermute | solution.py:261
  38.8 3.1 %collective-permute-start.3 = (f32[2,2048]{1,0:T(2,128)S(1)}, f32[2,2048]{1,0:T(2,128)S(1)}, u32[]{:S(2)}, u32[]{:S(2)}) collective-permute-start(f32[2,2048]{1,0:T(2,128)S(1)} %add.18), channel_id=1, source_target_pairs={{0,64},{64,0},{128,192},{192,128},{256,320},{320,256},{384,448},{4... | collective-permute-start | bytes 49160 | tf_op jit(solution)/shard_map/differences_over_replicas/ppermute | solution.py:237
  41.9 5.6 %collective-permute-start.4 = (f32[2,2048]{1,0:T(2,128)S(1)}, f32[2,2048]{1,0:T(2,128)S(1)}, u32[]{:S(2)}, u32[]{:S(2)}) collective-permute-start(f32[2,2048]{1,0:T(2,128)S(1)} %add.19), channel_id=1, source_target_pairs={{0,256},{64,320},{128,384},{192,448},{256,0},{320,64},{384,128},{4... | collective-permute-start | bytes 49160 | tf_op jit(solution)/shard_map/differences_over_replicas/ppermute | solution.py:237
  47.6 12.4 %collective-permute-start.5 = (s16[272,512]{1,0:T(8,128)(2,1)S(1)}, s16[272,512]{1,0:T(8,128)(2,1)S(1)}, u32[]{:S(2)}, u32[]{:S(2)}) collective-permute-start(s16[272,512]{1,0:T(8,128)(2,1)S(1)} %get-tuple-element.29), channel_id=1, source_target_pairs={{0,1},{1,0},{2,3},{3,2},{4,5},{5,4},{6,7},{7,6},{8,9},{9,8},{10,11... | collective-permute-start | bytes 835592 | tf_op jit(solution)/shard_map/near_along_line/ppermute | solution.py:261
  51.1 23.9 %collective-permute-start.7 = (s16[272,512]{1,0:T(8,128)(2,1)S(1)}, s16[272,512]{1,0:T(8,128)(2,1)S(1)}, u32[]{:S(2)}, u32[]{:S(2)}) collective-permute-start(s16[272,512]{1,0:T(8,128)(2,1)S(1)} %get-tuple-element.32), channel_id=1, source_target_pairs={{0,24},{1,25},{2,26},{3,27},{4,28},{5,29},{6,30},{7,31},{8,32},{9,... | collective-permute-start | bytes 835592 | tf_op jit(solution)/shard_map/far_along_ring/ppermute | solution.py:258
  56.9 24.1 %collective-permute-start.8 = (s16[272,512]{1,0:T(8,128)(2,1)S(1)}, s16[272,512]{1,0:T(8,128)(2,1)S(1)}, u32[]{:S(2)}, u32[]{:S(2)}) collective-permute-start(s16[272,512]{1,0:T(8,128)(2,1)S(1)} %get-tuple-element.33), channel_id=1, source_target_pairs={{0,40},{1,41},{2,42},{3,43},{4,44},{5,45},{6,46},{7,47},{8,48},{9,... | collective-permute-start | bytes 835592 | tf_op jit(solution)/shard_map/far_along_ring/ppermute | solution.py:258
  75.0 11.4 %collective-permute-start.11 = (f32[2,2048]{1,0:T(2,128)S(1)}, f32[2,2048]{1,0:T(2,128)S(1)}, u32[]{:S(2)}, u32[]{:S(2)}) collective-permute-start(f32[2,2048]{1,0:T(2,128)S(1)} %add.20), channel_id=1, source_target_pairs={{0,512},{64,576},{128,640},{192,704},{256,768},{320,832},{384,896}... | collective-permute-start | bytes 49160 | tf_op jit(solution)/shard_map/differences_over_replicas/ppermute | solution.py:237
  81.9 11.6 %collective-permute-start.9 = (s16[144,512]{1,0:T(8,128)(2,1)S(1)}, s16[144,512]{1,0:T(8,128)(2,1)S(1)}, u32[]{:S(2)}, u32[]{:S(2)}) collective-permute-start(s16[144,512]{1,0:T(8,128)(2,1)S(1)} %get-tuple-element.35), channel_id=1, source_target_pairs={{0,2},{1,3},{2,0},{3,1},{4,6},{5,7},{6,4},{7,5},{8,10},{9,11},{10,... | collective-permute-start | bytes 442376 | tf_op jit(solution)/shard_map/along_line/ppermute | solution.py:261
  94.2 17.4 %collective-permute-start.10 = (s16[80,512]{1,0:T(8,128)(2,1)S(1)}, s16[80,512]{1,0:T(8,128)(2,1)S(1)}, u32[]{:S(2)}, u32[]{:S(2)}) collective-permute-start(s16[80,512]{1,0:T(8,128)(2,1)S(1)} %get-tuple-element.37), channel_id=1, source_target_pairs={{0,4},{1,5},{2,6},{3,7},{4,0},{5,1},{6,2},{7,3},{8,12},{9,13},{10,... | collective-permute-start | bytes 245768 | tf_op jit(solution)/shard_map/along_line/ppermute | solution.py:261
